TPU v7x, 32 devices: a whole 2x2x4 slice. The times are simulated.
32 devices in a mesh: state: 2 (over x), row: 4 (over y, core), col: 4 (over z).
Axes of the slice: x: 2, y: 2, z: 4, core: 2. Of those that a mesh axis runs over, the one named last changes fastest.
Arguments:
- coeff_rows: bfloat16 [2048, 4096], P('row', 'state'), may hold values from -0.09375 to 0.09375
- coeff_cols: bfloat16 [4096, 4096], P('col', 'state'), may hold values from -0.09375 to 0.09375
- occupation: float32 [4096], P('state'), may hold values from 0.05 to 2
- send_list: int32 [2, 4, 4, 4, 2], P('state', 'row', 'col'), may hold values from 0 to 4
- row_phi: bfloat16 [2, 4, 4, 8, 256, 256], P('state', 'row', 'col'), may hold values from -6 to 6
- col_phi: bfloat16 [2, 4, 4, 8, 256, 256], P('state', 'row', 'col'), may hold values from -6 to 6
Outputs:
- density: float32 [2, 4, 4, 256], P('state', 'row', 'col')
Inputs may be any that keep to these rules, and one draw needn't show every extreme that they name: `send_list`: a value of 4 relays nothing.
All inputs are finite; a program needn't handle non-finite values.
Results may differ from a plain program's by a relative error of at most 0.004.
Values may be sent and summed in bfloat16 or wider, within the bound.
No kernel may reach another device: no remote copies, remote signals or barrier semaphores. Data moves between devices by JAX's collectives and lax.ppermute only.
A program may use at most 64 MiB of HBM per device.

v0:
```python
import jax
import jax.numpy as jnp
from jax import lax
from jax.sharding import PartitionSpec as P


def local(coeff_rows, coeff_cols, occupation, send_list, row_phi, col_phi):
    weighted = (coeff_rows.astype(jnp.float32) * occupation[None, :]).astype(jnp.bfloat16)
    partial_block = lax.dot_general(
        weighted, coeff_cols, (((1,), (1,)), ((), ())), preferred_element_type=jnp.float32
    )
    side = coeff_rows.shape[0] // lax.axis_size("state")
    summed = lax.psum(partial_block, "state")
    mine = lax.dynamic_slice_in_dim(summed, lax.axis_index("state") * side, side, 0)
    mine = mine.astype(jnp.bfloat16)
    count = mine.shape[1] // side
    tiles = mine.reshape(side, count, side).transpose(1, 0, 2)
    tiles = jnp.concatenate([tiles, jnp.zeros((1, side, side), jnp.bfloat16)], axis=0)
    picks = send_list[0, 0, 0]
    onehot = (picks[:, :, None] == jnp.arange(count + 1, dtype=jnp.int32)[None, None, :]).astype(
        jnp.bfloat16
    )
    outgoing = jnp.einsum(
        "jkt,tab->jkab", onehot, tiles, preferred_element_type=jnp.float32
    ).astype(jnp.bfloat16)
    received = lax.all_to_all(outgoing, "row", split_axis=0, concat_axis=0, tiled=True)
    received = received.reshape(-1, side, side)
    half = jnp.einsum(
        "tab,tbp->tap", received, col_phi[0, 0, 0], preferred_element_type=jnp.float32
    )
    density = jnp.sum(row_phi[0, 0, 0].astype(jnp.float32) * half, axis=(0, 1))
    return density.reshape(1, 1, 1, -1)


def solution(mesh):
    in_specs = (
        P("row", "state"),
        P("col", "state"),
        P("state"),
        P("state", "row", "col", None, None),
        P("state", "row", "col", None, None, None),
        P("state", "row", "col", None, None, None),
    )
    out_specs = P("state", "row", "col", None)
    return jax.shard_map(local, mesh=mesh, in_specs=in_specs, out_specs=out_specs, check_vma=False)
```

profile of v0, /device:TPU:0, one launch (start us, length us, event | category | flops | bytes accessed | tf_op | source)
XLA Modules:
  0.0 81.0 jit_solution(579882297609243278)
XLA Ops:
  0.0 0.0 copy-start
  0.0 6.6 %fusion = f32[512,1024]{1,0:T(8,128)} fusion(bf16[1024,2048]{1,0:T(8,128)(2,1)} %param.7, bf16[512,2048]{1,0:T(8,128)(2,1)} %param.6, f32[2048]{0:T(1024)} %param.8), kind=kOutput, calls=%fused_computation.1 | convolution fusion | flops 2150629376 | bytes 8396800 | tf_op jit(solution)/shard_map/dot_general | solution.py:9
  6.6 0.0 copy-start.1
  6.6 54.9 %all-reduce.2 = bf16[512,1024]{1,0:T(8,128)(2,1)S(1)} all-reduce(f32[512,1024]{1,0:T(8,128)} %fusion), channel_id=1, replica_groups=mesh['state'=2,'row'=4,'col'=4] {'state'}, use_global_device_ids=true, to_apply=%region_0.0 | all-reduce | flops 524288 | bytes 3145728 | tf_op jit(solution)/shard_map/psum | solution.py:13
  61.6 0.4 reshape.13
  62.0 0.0 copy-done.1
  62.0 0.6 convolution_convert_fusion
  62.6 0.0 copy-start.2
  62.6 0.1 copy.8
  62.7 17.2 %all_to_all.5 = bf16[4,2,256,256]{3,2,1,0:T(8,128)(2,1)S(1)} all-to-all(bf16[4,2,256,256]{3,2,1,0:T(8,128)(2,1)S(1)} %copy.8), channel_id=1, replica_groups=mesh['state'=2,'row'=4,'col'=4] {'row'}, dimensions={0} | all-to-all | bytes 2097152 | tf_op jit(solution)/shard_map/all_to_all | solution.py:26
  79.9 0.0 copy-done
  79.9 0.0 copy-done.2
  79.9 1.1 %fusion.1 = f32[256]{0:T(256)} fusion(bf16[8,256,256]{2,1,0:T(8,128)(2,1)S(1)} %bitcast.21, bf16[1,1,1,8,256,256]{5,4,3,2,1,0:T(8,128)(2,1)S(1)} %copy-done.2, bf16[1,1,1,8,256,256]{5,4,3,2,1,0:T(8,128)(2,1)S(1)} %copy-done), kind=kOutput, calls=%fused_computation.3 | convolution fusion | flops 270008064 | bytes 3146752 | tf_op jit(solution)/shard_map/tab,tbp->tap/dot_general | solution.py:28
  (1 shorter events, 0.0 us)
Async XLA Ops:
  0.0 79.9 %copy-start = (bf16[1,1,1,8,256,256]{5,4,3,2,1,0:T(8,128)(2,1)S(1)}, bf16[1,1,1,8,256,256]{5,4,3,2,1,0:T(8,128)(2,1)}, u32[]{:S(2)}) copy-start(bf16[1,1,1,8,256,256]{5,4,3,2,1,0:T(8,128)(2,1)} %param.11) | copy-start | bytes 3145732
  6.6 55.3 %copy-start.1 = (s32[1,1,1,4,2]{3,4,2,1,0:T(2,128)S(1)}, s32[1,1,1,4,2]{3,4,2,1,0:T(2,128)}, u32[]{:S(2)}) copy-start(s32[1,1,1,4,2]{3,4,2,1,0:T(2,128)} %param.9) | copy-start | bytes 100
  62.6 17.3 %copy-start.2 = (bf16[1,1,1,8,256,256]{5,4,3,2,1,0:T(8,128)(2,1)S(1)}, bf16[1,1,1,8,256,256]{5,4,3,2,1,0:T(8,128)(2,1)}, u32[]{:S(2)}) copy-start(bf16[1,1,1,8,256,256]{5,4,3,2,1,0:T(8,128)(2,1)} %param.10) | copy-start | bytes 3145732
where the time goes:
time: 81.2 us; the launch traced here: 81 us
  blocking collectives  72.1 us (89%)
  matrix products  8.25 us (10%)
    psum x1, blocking collectives, local(): summed = lax.psum(partial_block, 'state')  54.9 us
    all_to_all x1, blocking collectives, local(): lax.all_to_all(outgoing, 'row', split_axis=0, concat_axis=0, tiled=True)  17.2 us
    dot_general x1, matrix products, local(): lax.dot_general(weighted, coeff_cols, (((1,), (1,)), ((), ())), preferred...  6.64 us

commit v1 on v0

v1 whole, which is shorter than its diff:
```python
import functools

import jax
import jax.numpy as jnp
from jax import lax
from jax.experimental import pallas as pl
from jax.experimental.pallas import tpu as pltpu
from jax.sharding import PartitionSpec as P

CHUNKS = 2
VMEM_LIMIT = 24 * 1024 * 1024
NT = (((1,), (1,)), ((), ()))


def params():
    return pltpu.CompilerParams(vmem_limit_bytes=VMEM_LIMIT)


def product_kernel(block_ref, rows_ref, occ_ref, cols_ref, *refs):
    outs, weighted_ref = refs[:-1], refs[-1]

    @pl.when(pl.program_id(0) == 0)
    def _():
        weighted_ref[...] = (rows_ref[...].astype(jnp.float32) * occ_ref[...]).astype(jnp.bfloat16)

    total = lax.dot_general(weighted_ref[...], cols_ref[...], NT, preferred_element_type=jnp.float32)
    height = total.shape[0] // len(outs)
    for n, out in enumerate(outs):
        out[...] = total[n * height : (n + 1) * height].astype(out.dtype)


def product(block, coeff_rows, occupation, coeff_cols, side, pieces, dtype):
    states, width = coeff_rows.shape[1], coeff_cols.shape[0]
    step = min(256, width)
    height = side // pieces
    return pl.pallas_call(
        product_kernel,
        grid_spec=pltpu.PrefetchScalarGridSpec(
            num_scalar_prefetch=1,
            grid=(width // step,),
            in_specs=[
                pl.BlockSpec((side, states), lambda j, b: (b[0], 0)),
                pl.BlockSpec((1, states), lambda j, b: (0, 0)),
                pl.BlockSpec((step, states), lambda j, b: (j, 0)),
            ],
            out_specs=[pl.BlockSpec((height, step), lambda j, b: (0, j))] * pieces,
            scratch_shapes=[pltpu.VMEM((side, states), jnp.bfloat16)],
        ),
        out_shape=[jax.ShapeDtypeStruct((height, width), dtype)] * pieces,
        compiler_params=params(),
        cost_estimate=pl.CostEstimate(
            flops=2 * side * states * width, bytes_accessed=2 * states * (width + side), transcendentals=0
        ),
    )(block, coeff_rows, occupation, coeff_cols)


def pick_kernel(slots, picks_ref, own_ref, *refs):
    tiles_ref = refs[-1]
    owners = picks_ref.shape[0] // slots
    parts, outs = refs[: -1 - owners], refs[-1 - owners : -1]
    count, height, side = tiles_ref.shape[0] - 1, tiles_ref.shape[1], tiles_ref.shape[2]
    for t in range(count):
        cut = slice(t * side, (t + 1) * side)
        total = own_ref[:, cut]
        for part in parts:
            total = total + part[:, cut].astype(jnp.float32)
        tiles_ref[t] = total.astype(jnp.bfloat16)
    tiles_ref[count] = jnp.zeros((height, side), jnp.bfloat16)
    for d, out in enumerate(outs):
        for k in range(slots):
            out[k] = tiles_ref[picks_ref[d * slots + k]]


def pick(picks, own, parts, side, owners, slots):
    height, width = own.shape
    return pl.pallas_call(
        functools.partial(pick_kernel, slots),
        in_specs=[pl.BlockSpec(memory_space=pltpu.SMEM)]
        + [pl.BlockSpec(memory_space=pltpu.VMEM)] * (1 + len(parts)),
        out_specs=[pl.BlockSpec(memory_space=pltpu.VMEM)] * owners,
        out_shape=[jax.ShapeDtypeStruct((slots, height, side), jnp.bfloat16)] * owners,
        scratch_shapes=[pltpu.VMEM((width // side + 1, height, side), jnp.bfloat16)],
        compiler_params=params(),
        cost_estimate=pl.CostEstimate(flops=height * width, bytes_accessed=8 * height * width, transcendentals=0),
    )(picks, own, *parts)


def contract_kernel(sources_ref, before_ref, row_phi_ref, col_phi_ref, *refs):
    gots, out = refs[:-1], refs[-1]
    density = before_ref[...]
    for d, got in enumerate(gots):
        slots = got.shape[0]
        for k in range(slots):
            m = sources_ref[d] * slots + k
            half = jnp.dot(got[k], col_phi_ref[m], preferred_element_type=jnp.float32)
            density += jnp.sum(row_phi_ref[m].astype(jnp.float32) * half, axis=0, keepdims=True)
    out[...] = density


def contract(sources, before, row_phi, col_phi, gots, chunk):
    received, side, points = col_phi.shape
    slots, height, _ = gots[0].shape
    return pl.pallas_call(
        contract_kernel,
        grid=(1,),
        in_specs=[
            pl.BlockSpec(memory_space=pltpu.SMEM),
            pl.BlockSpec((1, points), lambda j: (0, 0)),
            pl.BlockSpec((received, height, points), lambda j: (0, chunk, 0)),
            pl.BlockSpec((received, side, points), lambda j: (0, 0, 0)),
        ]
        + [pl.BlockSpec((slots, height, side), lambda j: (0, 0, 0))] * len(gots),
        out_specs=pl.BlockSpec((1, points), lambda j: (0, 0)),
        out_shape=jax.ShapeDtypeStruct((1, points), jnp.float32),
        compiler_params=params(),
        cost_estimate=pl.CostEstimate(
            flops=2 * received * height * side * points, bytes_accessed=2 * received * side * points, transcendentals=0
        ),
    )(sources, before, row_phi, col_phi, *gots)


def swap(value, axis, d):
    return lax.ppermute(value, axis, [(i, i ^ d) for i in range(lax.axis_size(axis))])


def local(coeff_rows, coeff_cols, occupation, send_list, row_phi, col_phi):
    states, owners = lax.axis_size("state"), lax.axis_size("row")
    state, row = lax.axis_index("state"), lax.axis_index("row")
    side = coeff_rows.shape[0] // states
    slots = send_list.shape[-1]
    row_phi, col_phi = row_phi[0, 0, 0], col_phi[0, 0, 0]
    occupation = occupation[None, :]
    sources = jnp.bitwise_xor(row, jnp.arange(owners, dtype=jnp.int32))
    picks = send_list[0, 0, 0][sources].reshape(-1)

    arrived = [[] for _ in range(CHUNKS)]
    for d in range(1, states):
        target = jnp.bitwise_xor(state, d).astype(jnp.int32)[None]
        sent = product(target, coeff_rows, occupation, coeff_cols, side, CHUNKS, jnp.bfloat16)
        for c in range(CHUNKS):
            arrived[c].append(swap(sent[c], "state", d))
    own = product(state.astype(jnp.int32)[None], coeff_rows, occupation, coeff_cols, side, CHUNKS, jnp.float32)

    density = jnp.zeros((1, row_phi.shape[-1]), jnp.float32)
    for c in range(CHUNKS):
        outgoing = pick(picks, own[c], arrived[c], side, owners, slots)
        gots = [outgoing[0]] + [swap(outgoing[d], "row", d) for d in range(1, owners)]
        density = contract(sources, density, row_phi, col_phi, gots, c)
    return density.reshape(1, 1, 1, -1)


def solution(mesh):
    in_specs = (
        P("row", "state"),
        P("col", "state"),
        P("state"),
        P("state", "row", "col", None, None),
        P("state", "row", "col", None, None, None),
        P("state", "row", "col", None, None, None),
    )
    out_specs = P("state", "row", "col", None)
    return jax.shard_map(local, mesh=mesh, in_specs=in_specs, out_specs=out_specs, check_vma=False)
```

time: 81.2 us -> 35.1 us (0.43)
  blocking collectives: 72.1 us -> 0 us
  waiting for transfers between devices: 0 us -> 10.9 us
  Pallas kernels: 0 us -> 9.09 us
  matrix products: 8.25 us -> 0 us
  starting transfers between devices: 0 us -> 7.24 us
  local copies, waits for them, and re-layouts: 0.57 us -> 7.45 us
    psum x1 -> x0, blocking collectives: 54.9 us -> none  [local(): summed = lax.psum(partial_block, 'state')]
    all_to_all x1 -> x0, blocking collectives: 17.2 us -> none  [local(): lax.all_to_all(outgoing, 'row', split_axis=0, concat_axis=0, tiled=True)]
    ppermute x0 -> x8, waiting for transfers between devices: none -> 10.9 us  [swap(): lax.ppermute(value, axis, [(i, i ^ d) for i in range(lax.axis_size(axis))])]
    pallas_call x0 -> x6, Pallas kernels: none -> 9.09 us  [the longest x2 5.06 us: product(): pl.pallas_call(product_kernel, grid_spec=pltpu.PrefetchScalarGridSpec(num...]
    dot_general x3 -> x0, matrix products: 8.25 us -> none  [the longest x1 6.64 us: local(): lax.dot_general(weighted, coeff_cols, (((1,), (1,)), ((), ())), preferred...]
    ppermute x0 -> x8, starting transfers between devices: none -> 7.24 us  [swap(): lax.ppermute(value, axis, [(i, i ^ d) for i in range(lax.axis_size(axis))])]
    unnamed x6 -> x18, local copies, waits for them, and re-layouts: 0.01 us -> 6.71 us
  transfers between devices with their start and end apart: 0 -> 8, of which waited for: 0 -> 6; matrix products, arithmetic and copies ran while one was open for 0% -> 2% of each run, Pallas kernels for 0% -> 14%
where the time goes in v1:
time: 35.1 us; the launch traced here: 34.8 us
  waiting for transfers between devices  10.9 us (31%)
  Pallas kernels  9.09 us (26%)
  local copies, waits for them, and re-layouts  7.45 us (21%)
  starting transfers between devices  7.24 us (21%)
    ppermute x8, waiting for transfers between devices, swap(): lax.ppermute(value, axis, [(i, i ^ d) for i in range(lax.axis_size(axis))])  10.9 us
    ppermute x8, starting transfers between devices, swap(): lax.ppermute(value, axis, [(i, i ^ d) for i in range(lax.axis_size(axis))])  7.24 us
    unnamed x18, local copies, waits for them, and re-layouts  6.71 us
    pallas_call x2, Pallas kernels, product(): pl.pallas_call(product_kernel, grid_spec=pltpu.PrefetchScalarGridSpec(num...  5.06 us
    pallas_call x2, Pallas kernels, contract(): pl.pallas_call(contract_kernel, grid=(1,), in_specs=[pl.BlockSpec(memory_...  2.33 us
    pallas_call x2, Pallas kernels, pick(): pl.pallas_call(functools.partial(pick_kernel, slots), in_specs=[pl.BlockS...  1.69 us
  transfers between devices with their start and end apart: 8, of which 6 were waited for; matrix products, arithmetic and copies ran while one was open for 2% of the time, Pallas kernels for 14%

profile of v1, /device:TPU:0, one launch (start us, length us, event | category | flops | bytes accessed | tf_op | source)
XLA Modules:
  0.0 34.8 jit_solution(18266544726320981862)
XLA Ops:
  0.0 2.2 %copy-done = bf16[1024,2048]{1,0:T(8,128)(2,1)S(1)} copy-done((bf16[1024,2048]{1,0:T(8,128)(2,1)S(1)}, bf16[1024,2048]{1,0:T(8,128)(2,1)}, u32[]{:S(2)}) %copy-start) | copy-done | bytes 4194328
  2.2 1.6 %copy-done.2 = bf16[512,2048]{1,0:T(8,128)(2,1)S(1)} copy-done((bf16[512,2048]{1,0:T(8,128)(2,1)S(1)}, bf16[512,2048]{1,0:T(8,128)(2,1)}, u32[]{:S(2)}) %copy-start.2) | copy-done | bytes 2097176
  3.8 0.7 %copy-done.6 = f32[2048]{0:T(1024)S(1)} copy-done((f32[2048]{0:T(1024)S(1)}, f32[2048]{0:T(1024)}, u32[]{:S(2)}) %copy-start.6) | copy-done | bytes 8216
  4.5 2.9 %shard_map.65 = (bf16[128,1024]{1,0:T(8,128)(2,1)}, bf16[128,1024]{1,0:T(8,128)(2,1)}) custom-call(s32[1]{0:T(128)} %bitcast.6.block_ref, bf16[512,2048]{1,0:T(8,128)(2,1)S(1)} %copy-done.2, f32[1,2048]{1,0:T(1,128)S(1)} %bitcast.13, bf16[1024,2048]{1,0:T(8,128)(2,1)S(1)} %copy-done), custom_call_target="tpu_custom_call" | custom-call | flops 1073741824 | bytes 5242880 | tf_op jit(solution)/shard_map/pallas_call | solution.py:36
  7.4 2.9 %collective-permute-start = (bf16[128,1024]{1,0:T(8,128)(2,1)}, bf16[128,1024]{1,0:T(8,128)(2,1)}, u32[]{:S(2)}, u32[]{:S(2)}) collective-permute-start(bf16[128,1024]{1,0:T(8,128)(2,1)} %get-tuple-element.18), channel_id=1, source_target_pairs={{0,16},{16,0},{1,17},{17,1},{2,18},{18,2},{3,19},{19,3},{4,20},{20... | collective-permute-start | bytes 786440 | tf_op jit(solution)/shard_map/ppermute | solution.py:123
  10.4 0.1 copy.8
  10.5 0.6 %gather_fusion = s32[4,2]{1,0:T(4,128)S(1)} fusion(s32[4,2]{1,0:T(4,128)S(1)} %copy.8, s32[1024]{0:T(1024)S(1)} %pad_clamp_fusion), kind=kCustom, calls=%fused_computation | custom fusion | bytes 80 | tf_op jit(solution)/shard_map/gather | solution.py:134
  11.1 0.1 reshape.22.picks_ref
  11.1 2.2 %copy-done.1 = bf16[1024,2048]{1,0:T(8,128)(2,1)S(1)} copy-done((bf16[1024,2048]{1,0:T(8,128)(2,1)S(1)}, bf16[1024,2048]{1,0:T(8,128)(2,1)}, u32[]{:S(2)}) %copy-start.1) | copy-done | bytes 4194328
  13.3 2.2 %shard_map.64 = (f32[128,1024]{1,0:T(8,128)S(1)}, f32[128,1024]{1,0:T(8,128)S(1)}) custom-call(s32[1]{0:T(128)} %bitcast.4.block_ref, bf16[512,2048]{1,0:T(8,128)(2,1)S(1)} %copy-done.3, f32[1,2048]{1,0:T(1,128)S(1)} %bitcast.14, bf16[1024,2048]{1,0:T(8,128)(2,1)S(1)} %copy-done.1), custom_call_target="tpu_custom_call" | custom-call | flops 1073741824 | bytes 5242880 | tf_op jit(solution)/shard_map/pallas_call | solution.py:36
  15.5 2.3 %collective-permute-done.refs_0_ = bf16[128,1024]{1,0:T(8,128)(2,1)} collective-permute-done((bf16[128,1024]{1,0:T(8,128)(2,1)}, bf16[128,1024]{1,0:T(8,128)(2,1)}, u32[]{:S(2)}, u32[]{:S(2)}) %collective-permute-start) | collective-permute-done | bytes 262176 | tf_op jit(solution)/shard_map/ppermute | solution.py:123
  17.8 1.1 %shard_map.66 = (bf16[2,128,256]{2,1,0:T(8,128)(2,1)S(1)}, bf16[2,128,256]{2,1,0:T(8,128)(2,1)S(1)}, bf16[2,128,256]{2,1,0:T(8,128)(2,1)S(1)}, bf16[2,128,256]{2,1,0:T(8,128)(2,1)S(1)}) custom-call(s32[8]{0:T(128)S(1)} %reshape.22.picks_ref, f32[128,1024]{1,0:T(8,128)S(1)} %get-tuple-element.17.own_ref, bf16[128,1024]{1,0:T(8,128)(2,1)} %collective-permute-done.refs_0_), custom_call_target="tpu_custom_call" | custom-call | flops 131072 | bytes 1048576 | tf_op jit(solution)/shard_map/pallas_call | solution.py:76
  18.9 0.1 collective-permute-start.1
  18.9 2.1 %collective-permute-start.2 = (bf16[2,128,256]{2,1,0:T(8,128)(2,1)S(1)}, bf16[2,128,256]{2,1,0:T(8,128)(2,1)S(1)}, u32[]{:S(2)}, u32[]{:S(2)}) collective-permute-start(bf16[2,128,256]{2,1,0:T(8,128)(2,1)S(1)} %get-tuple-element.21), channel_id=1, source_target_pairs={{0,8},{4,12},{8,0},{12,4},{1,9},{5,13},{9,1},{13,5},{2,10},{6,14},... | collective-permute-start | bytes 393224 | tf_op jit(solution)/shard_map/ppermute | solution.py:123
  21.2 1.3 %collective-permute-done.4.refs_0_ = bf16[128,1024]{1,0:T(8,128)(2,1)S(1)} collective-permute-done((bf16[128,1024]{1,0:T(8,128)(2,1)}, bf16[128,1024]{1,0:T(8,128)(2,1)S(1)}, u32[]{:S(2)}, u32[]{:S(2)}) %collective-permute-start.4) | collective-permute-done | bytes 262176 | tf_op jit(solution)/shard_map/ppermute | solution.py:123
  22.5 0.6 %shard_map.68 = (bf16[2,128,256]{2,1,0:T(8,128)(2,1)S(1)}, bf16[2,128,256]{2,1,0:T(8,128)(2,1)S(1)}, bf16[2,128,256]{2,1,0:T(8,128)(2,1)S(1)}, bf16[2,128,256]{2,1,0:T(8,128)(2,1)S(1)}) custom-call(s32[8]{0:T(128)S(1)} %reshape.22.picks_ref, f32[128,1024]{1,0:T(8,128)S(1)} %get-tuple-element.23.own_ref, bf16[128,1024]{1,0:T(8,128)(2,1)S(1)} %collective-permute-done.4.refs_0_), custom_call_target="tpu_custom_call" | custom-call | flops 131072 | bytes 1048576 | tf_op jit(solution)/shard_map/pallas_call | solution.py:76
  23.1 0.1 collective-permute-start.5
  23.2 1.8 %collective-permute-start.6 = (bf16[2,128,256]{2,1,0:T(8,128)(2,1)S(1)}, bf16[2,128,256]{2,1,0:T(8,128)(2,1)S(1)}, u32[]{:S(2)}, u32[]{:S(2)}) collective-permute-start(bf16[2,128,256]{2,1,0:T(8,128)(2,1)S(1)} %get-tuple-element.27), channel_id=1, source_target_pairs={{0,8},{4,12},{8,0},{12,4},{1,9},{5,13},{9,1},{13,5},{2,10},{6,14},... | collective-permute-start | bytes 393224 | tf_op jit(solution)/shard_map/ppermute | solution.py:123
  25.1 0.3 collective-permute-done.2.refs_2_
  25.4 2.3 %collective-permute-done.3.refs_3_ = bf16[2,128,256]{2,1,0:T(8,128)(2,1)S(1)} collective-permute-done((bf16[2,128,256]{2,1,0:T(8,128)(2,1)S(1)}, bf16[2,128,256]{2,1,0:T(8,128)(2,1)S(1)}, u32[]{:S(2)}, u32[]{:S(2)}) %collective-permute-start.3) | collective-permute-done | bytes 131104 | tf_op jit(solution)/shard_map/ppermute | solution.py:123
  27.7 0.9 %shard_map.67.before_ref = f32[1,256]{1,0:T(1,128)S(1)} custom-call(s32[4]{0:T(128)S(1)} %iota_xor_fusion.sources_ref, f32[1,256]{1,0:T(1,128)S(1)} %broadcast_in_dim.13.before_ref, bf16[8,256,256]{2,1,0:T(8,128)(2,1)S(1)} %bitcast.9, bf16[8,256,256]{2,1,0:T(8,128)(2,1)S(1)} %bitcast.11, bf16[2,128,256]{2,1,0:T(8,128)(2,1)S(1)} %get-tuple-element.19.refs_0_, ...), custom_call_target="tpu_custom_call" | custom-call | flops 134217728 | bytes 1048576 | tf_op jit(solution)/shard_map/pallas_call | solution.py:103
  28.6 2.4 %collective-permute-done.6.refs_2_ = bf16[2,128,256]{2,1,0:T(8,128)(2,1)S(1)} collective-permute-done((bf16[2,128,256]{2,1,0:T(8,128)(2,1)S(1)}, bf16[2,128,256]{2,1,0:T(8,128)(2,1)S(1)}, u32[]{:S(2)}, u32[]{:S(2)}) %collective-permute-start.6) | collective-permute-done | bytes 131104 | tf_op jit(solution)/shard_map/ppermute | solution.py:123
  31.1 2.3 %collective-permute-done.7.refs_3_ = bf16[2,128,256]{2,1,0:T(8,128)(2,1)S(1)} collective-permute-done((bf16[2,128,256]{2,1,0:T(8,128)(2,1)S(1)}, bf16[2,128,256]{2,1,0:T(8,128)(2,1)S(1)}, u32[]{:S(2)}, u32[]{:S(2)}) %collective-permute-start.7) | collective-permute-done | bytes 131104 | tf_op jit(solution)/shard_map/ppermute | solution.py:123
  33.3 1.4 %shard_map.69 = f32[1,256]{1,0:T(1,128)} custom-call(s32[4]{0:T(128)S(1)} %iota_xor_fusion.sources_ref, f32[1,256]{1,0:T(1,128)S(1)} %shard_map.67.before_ref, bf16[8,256,256]{2,1,0:T(8,128)(2,1)S(1)} %bitcast.10, bf16[8,256,256]{2,1,0:T(8,128)(2,1)S(1)} %bitcast.12, bf16[2,128,256]{2,1,0:T(8,128)(2,1)S(1)} %get-tuple-element.25.refs_0_, ...), custom_call_target="tpu_custom_call" | custom-call | flops 134217728 | bytes 1048576 | tf_op jit(solution)/shard_map/pallas_call | solution.py:103
  (23 shorter events, 0.2 us)
Async XLA Ops:
  0.0 11.1 %copy-start.7 = (f32[2048]{0:T(1024)S(1)}, f32[2048]{0:T(1024)}, u32[]{:S(2)}) copy-start(f32[2048]{0:T(1024)} %param.8) | copy-start | bytes 24580
  0.0 10.4 %copy-start.8 = (s32[1,1,1,4,2]{3,4,2,1,0:T(2,128)S(1)}, s32[1,1,1,4,2]{3,4,2,1,0:T(2,128)}, u32[]{:S(2)}) copy-start(s32[1,1,1,4,2]{3,4,2,1,0:T(2,128)} %param.9) | copy-start | bytes 100
  0.0 2.2 %copy-start = (bf16[1024,2048]{1,0:T(8,128)(2,1)S(1)}, bf16[1024,2048]{1,0:T(8,128)(2,1)}, u32[]{:S(2)}) copy-start(bf16[1024,2048]{1,0:T(8,128)(2,1)} %cols_ref.3) | copy-start | bytes 12582916
  2.2 1.6 %copy-start.2 = (bf16[512,2048]{1,0:T(8,128)(2,1)S(1)}, bf16[512,2048]{1,0:T(8,128)(2,1)}, u32[]{:S(2)}) copy-start(bf16[512,2048]{1,0:T(8,128)(2,1)} %rows_ref.3) | copy-start | bytes 6291460
  3.8 0.7 %copy-start.6 = (f32[2048]{0:T(1024)S(1)}, f32[2048]{0:T(1024)}, u32[]{:S(2)}) copy-start(f32[2048]{0:T(1024)} %param.8) | copy-start | bytes 24580
  4.5 6.6 %copy-start.3 = (bf16[512,2048]{1,0:T(8,128)(2,1)S(1)}, bf16[512,2048]{1,0:T(8,128)(2,1)}, u32[]{:S(2)}) copy-start(bf16[512,2048]{1,0:T(8,128)(2,1)} %rows_ref.3) | copy-start | bytes 6291460
  4.5 23.2 %copy-start.4 = (bf16[1,1,1,8,256,256]{5,4,3,2,1,0:T(8,128)(2,1)S(1)}, bf16[1,1,1,8,256,256]{5,4,3,2,1,0:T(8,128)(2,1)}, u32[]{:S(2)}) copy-start(bf16[1,1,1,8,256,256]{5,4,3,2,1,0:T(8,128)(2,1)} %param.10) | copy-start | bytes 3145732
  7.4 10.4 %collective-permute-start = (bf16[128,1024]{1,0:T(8,128)(2,1)}, bf16[128,1024]{1,0:T(8,128)(2,1)}, u32[]{:S(2)}, u32[]{:S(2)}) collective-permute-start(bf16[128,1024]{1,0:T(8,128)(2,1)} %get-tuple-element.18), channel_id=1, source_target_pairs={{0,16},{16,0},{1,17},{17,1},{2,18},{18,2},{3,19},{19,3},{4,20},{20... | collective-permute-start | bytes 786440 | tf_op jit(solution)/shard_map/ppermute | solution.py:123
  10.3 12.1 %collective-permute-start.4 = (bf16[128,1024]{1,0:T(8,128)(2,1)}, bf16[128,1024]{1,0:T(8,128)(2,1)S(1)}, u32[]{:S(2)}, u32[]{:S(2)}) collective-permute-start(bf16[128,1024]{1,0:T(8,128)(2,1)} %get-tuple-element.24), channel_id=1, source_target_pairs={{0,16},{16,0},{1,17},{17,1},{2,18},{18,2},{3,19},{19,3},{4,20},{20... | collective-permute-start | bytes 786440 | tf_op jit(solution)/shard_map/ppermute | solution.py:123
  11.1 2.2 %copy-start.1 = (bf16[1024,2048]{1,0:T(8,128)(2,1)S(1)}, bf16[1024,2048]{1,0:T(8,128)(2,1)}, u32[]{:S(2)}) copy-start(bf16[1024,2048]{1,0:T(8,128)(2,1)} %cols_ref.3) | copy-start | bytes 12582916
  13.3 14.4 %copy-start.5 = (bf16[1,1,1,8,256,256]{5,4,3,2,1,0:T(8,128)(2,1)S(1)}, bf16[1,1,1,8,256,256]{5,4,3,2,1,0:T(8,128)(2,1)}, u32[]{:S(2)}) copy-start(bf16[1,1,1,8,256,256]{5,4,3,2,1,0:T(8,128)(2,1)} %param.11) | copy-start | bytes 3145732
  18.9 6.2 %collective-permute-start.1 = (bf16[2,128,256]{2,1,0:T(8,128)(2,1)S(1)}, bf16[2,128,256]{2,1,0:T(8,128)(2,1)S(1)}, u32[]{:S(2)}, u32[]{:S(2)}) collective-permute-start(bf16[2,128,256]{2,1,0:T(8,128)(2,1)S(1)} %get-tuple-element.20), channel_id=1, source_target_pairs={{0,4},{4,0},{8,12},{12,8},{1,5},{5,1},{9,13},{13,9},{2,6},{6,2},{1... | collective-permute-start | bytes 393224 | tf_op jit(solution)/shard_map/ppermute | solution.py:123
  18.9 6.5 %collective-permute-start.2 = (bf16[2,128,256]{2,1,0:T(8,128)(2,1)S(1)}, bf16[2,128,256]{2,1,0:T(8,128)(2,1)S(1)}, u32[]{:S(2)}, u32[]{:S(2)}) collective-permute-start(bf16[2,128,256]{2,1,0:T(8,128)(2,1)S(1)} %get-tuple-element.21), channel_id=1, source_target_pairs={{0,8},{4,12},{8,0},{12,4},{1,9},{5,13},{9,1},{13,5},{2,10},{6,14},... | collective-permute-start | bytes 393224 | tf_op jit(solution)/shard_map/ppermute | solution.py:123
  21.1 6.6 %collective-permute-start.3 = (bf16[2,128,256]{2,1,0:T(8,128)(2,1)S(1)}, bf16[2,128,256]{2,1,0:T(8,128)(2,1)S(1)}, u32[]{:S(2)}, u32[]{:S(2)}) collective-permute-start(bf16[2,128,256]{2,1,0:T(8,128)(2,1)S(1)} %get-tuple-element.22), channel_id=1, source_target_pairs={{0,12},{4,8},{8,4},{12,0},{1,13},{5,9},{9,5},{13,1},{2,14},{6,10},... | collective-permute-start | bytes 393224 | tf_op jit(solution)/shard_map/ppermute | solution.py:123
  23.1 5.5 %collective-permute-start.5 = (bf16[2,128,256]{2,1,0:T(8,128)(2,1)S(1)}, bf16[2,128,256]{2,1,0:T(8,128)(2,1)S(1)}, u32[]{:S(2)}, u32[]{:S(2)}) collective-permute-start(bf16[2,128,256]{2,1,0:T(8,128)(2,1)S(1)} %get-tuple-element.26), channel_id=1, source_target_pairs={{0,4},{4,0},{8,12},{12,8},{1,5},{5,1},{9,13},{13,9},{2,6},{6,2},{1... | collective-permute-start | bytes 393224 | tf_op jit(solution)/shard_map/ppermute | solution.py:123
  23.2 7.9 %collective-permute-start.6 = (bf16[2,128,256]{2,1,0:T(8,128)(2,1)S(1)}, bf16[2,128,256]{2,1,0:T(8,128)(2,1)S(1)}, u32[]{:S(2)}, u32[]{:S(2)}) collective-permute-start(bf16[2,128,256]{2,1,0:T(8,128)(2,1)S(1)} %get-tuple-element.27), channel_id=1, source_target_pairs={{0,8},{4,12},{8,0},{12,4},{1,9},{5,13},{9,1},{13,5},{2,10},{6,14},... | collective-permute-start | bytes 393224 | tf_op jit(solution)/shard_map/ppermute | solution.py:123
  25.0 8.3 %collective-permute-start.7 = (bf16[2,128,256]{2,1,0:T(8,128)(2,1)S(1)}, bf16[2,128,256]{2,1,0:T(8,128)(2,1)S(1)}, u32[]{:S(2)}, u32[]{:S(2)}) collective-permute-start(bf16[2,128,256]{2,1,0:T(8,128)(2,1)S(1)} %get-tuple-element.28), channel_id=1, source_target_pairs={{0,12},{4,8},{8,4},{12,0},{1,13},{5,9},{9,5},{13,1},{2,14},{6,10},... | collective-permute-start | bytes 393224 | tf_op jit(solution)/shard_map/ppermute | solution.py:123

commit v2 on v0

v2 whole, which is shorter than its diff:
```python
import functools

import jax
import jax.numpy as jnp
from jax import lax
from jax.experimental import pallas as pl
from jax.experimental.pallas import tpu as pltpu
from jax.sharding import PartitionSpec as P

EIGHTHS = (3, 3, 2)
MIB = 1024 * 1024
NT = (((1,), (1,)), ((), ()))
VMEM = pl.BlockSpec(memory_space=pltpu.VMEM)
SMEM = pl.BlockSpec(memory_space=pltpu.SMEM)
HBM = pl.BlockSpec(memory_space=pltpu.HBM)


def params(mib):
    return pltpu.CompilerParams(vmem_limit_bytes=mib * MIB)


def first_kernel(rows_hbm, occ_hbm, cols_hbm, out, rows_ref, occ_ref, cols_ref, occ_sem, rows_sem, cols_sem):
    side, states = rows_ref.shape
    height = cols_ref.shape[1]
    block = pl.multiple_of((lax.axis_index("state") ^ 1) * side, side)
    copies = [
        pltpu.make_async_copy(occ_hbm, occ_ref, occ_sem),
        pltpu.make_async_copy(rows_hbm.at[pl.ds(block, side)], rows_ref, rows_sem),
        pltpu.make_async_copy(cols_hbm.at[:, pl.ds(0, height)], cols_ref, cols_sem),
    ]
    for copy in copies:
        copy.start()
    copies[0].wait()
    copies[1].wait()
    weighted = (rows_ref[...].astype(jnp.float32) * occ_ref[...]).astype(jnp.bfloat16)
    copies[2].wait()
    total = lax.dot_general(cols_ref[...].reshape(-1, states), weighted, NT, preferred_element_type=jnp.float32)
    out[...] = total.reshape(out.shape).astype(out.dtype)


def first(height, coeff_rows, occupation, coeff_cols, side):
    count, _, states = coeff_cols.shape
    operands = (coeff_rows, occupation, coeff_cols)
    return pl.pallas_call(
        first_kernel,
        in_specs=[HBM] * 3,
        out_specs=VMEM,
        out_shape=jax.ShapeDtypeStruct((count, height, side), jnp.bfloat16),
        scratch_shapes=[
            pltpu.VMEM((side, states), jnp.bfloat16),
            pltpu.VMEM((1, states), jnp.float32),
            pltpu.VMEM((count, height, states), jnp.bfloat16),
            pltpu.SemaphoreType.DMA,
            pltpu.SemaphoreType.DMA,
            pltpu.SemaphoreType.DMA,
        ],
        compiler_params=params(16),
        cost_estimate=pl.CostEstimate(
            flops=2 * side * states * count * height,
            bytes_accessed=2 * states * (count * height + side),
            transcendentals=0,
        ),
    )(*(pltpu.with_memory_space_constraint(x, pltpu.HBM) for x in operands))


def rest_kernel(heights, rows_ref, occ_ref, cols_ref, *refs):
    outs, weighted_ref = list(refs[:-1]), refs[-1]
    groups, side = weighted_ref.shape[0] // cols_ref.shape[1], cols_ref.shape[1]
    states = weighted_ref.shape[1]
    state = lax.axis_index("state")
    for d in range(groups):
        rows = rows_ref[pl.ds(pl.multiple_of((state ^ d) * side, side), side)]
        weighted_ref[d * side : (d + 1) * side] = (rows.astype(jnp.float32) * occ_ref[...]).astype(jnp.bfloat16)
    start = 0
    for c, height in enumerate(heights):
        cols = cols_ref[:, start : start + height].reshape(-1, states)
        total = lax.dot_general(cols, weighted_ref[...], NT, preferred_element_type=jnp.float32)
        for d in range(groups):
            if (c, d) != (0, 1):
                out = outs.pop(0)
                out[...] = total[:, d * side : (d + 1) * side].reshape(out.shape).astype(out.dtype)
        start += height


def rest(heights, coeff_rows, occupation, coeff_cols, side):
    count, _, states = coeff_cols.shape
    groups = coeff_rows.shape[0] // side
    keys = [(c, d) for c in range(len(heights)) for d in range(groups) if (c, d) != (0, 1)]
    outs = pl.pallas_call(
        functools.partial(rest_kernel, heights),
        in_specs=[VMEM] * 3,
        out_specs=[VMEM] * len(keys),
        out_shape=[
            jax.ShapeDtypeStruct((count, heights[c], side), jnp.bfloat16 if d else jnp.float32) for c, d in keys
        ],
        scratch_shapes=[pltpu.VMEM((groups * side, states), jnp.bfloat16)],
        compiler_params=params(16),
        cost_estimate=pl.CostEstimate(
            flops=2 * groups * side * states * count * side,
            bytes_accessed=2 * states * (count + groups) * side,
            transcendentals=0,
        ),
    )(coeff_rows, occupation, coeff_cols)
    return dict(zip(keys, outs))


def pick_kernel(picks_ref, own_ref, *refs):
    tiles_ref = refs[-1]
    owners, slots = picks_ref.shape
    row = lax.axis_index("row")
    parts, outs = refs[: -1 - owners], refs[-1 - owners : -1]
    count = own_ref.shape[0]
    total = own_ref[...]
    for part in parts:
        total = total + part[...].astype(jnp.float32)
    tiles_ref[:count] = total.astype(jnp.bfloat16)
    tiles_ref[count] = jnp.zeros(tiles_ref.shape[1:], jnp.bfloat16)
    for d, out in enumerate(outs):
        for k in range(slots):
            out[k] = tiles_ref[picks_ref[row ^ d, k]]


def pick(picks, own, parts):
    count, height, side = own.shape
    owners, slots = picks.shape
    return pl.pallas_call(
        pick_kernel,
        in_specs=[SMEM] + [VMEM] * (1 + len(parts)),
        out_specs=[VMEM] * owners,
        out_shape=[jax.ShapeDtypeStruct((slots, height, side), jnp.bfloat16)] * owners,
        scratch_shapes=[pltpu.VMEM((count + 1, height, side), jnp.bfloat16)],
        compiler_params=params(8),
        cost_estimate=pl.CostEstimate(
            flops=count * height * side, bytes_accessed=8 * count * height * side, transcendentals=0
        ),
    )(picks, own, *parts)


def contract_kernel(start, before_ref, row_phi_ref, col_phi_ref, *refs):
    gots, out = refs[:-1], refs[-1]
    row = lax.axis_index("row")
    cut = pl.ds(start, gots[0].shape[1])
    density = before_ref[...]
    for d, got in enumerate(gots):
        slots = got.shape[0]
        for k in range(slots):
            m = (row ^ d) * slots + k
            half = jnp.dot(got[k], row_phi_ref[m], preferred_element_type=jnp.float32)
            density += jnp.sum(col_phi_ref[m, cut].astype(jnp.float32) * half, axis=0, keepdims=True)
    out[...] = density


def contract(before, row_phi, col_phi, gots, start):
    received, side, points = col_phi.shape
    height = gots[0].shape[1]
    return pl.pallas_call(
        functools.partial(contract_kernel, start),
        in_specs=[VMEM] * (3 + len(gots)),
        out_specs=VMEM,
        out_shape=jax.ShapeDtypeStruct((1, points), jnp.float32),
        compiler_params=params(8),
        cost_estimate=pl.CostEstimate(
            flops=2 * received * height * side * points, bytes_accessed=2 * received * side * points, transcendentals=0
        ),
    )(before, row_phi, col_phi, *gots)


def swap(value, axis, d):
    return lax.ppermute(value, axis, [(i, i ^ d) for i in range(lax.axis_size(axis))])


def local(coeff_rows, coeff_cols, occupation, send_list, row_phi, col_phi):
    states, owners = lax.axis_size("state"), lax.axis_size("row")
    side = coeff_rows.shape[0] // states
    heights = [side * n // 8 for n in EIGHTHS]
    row_phi, col_phi, picks = row_phi[0, 0, 0], col_phi[0, 0, 0], send_list[0, 0, 0]
    factors = coeff_rows, occupation[None, :], coeff_cols.reshape(-1, side, coeff_cols.shape[1]), side

    early = first(heights[0], *factors)
    parts = rest(heights, *factors)
    parts[0, 1] = early
    arrived = [[swap(parts[c, d], "state", d) for d in range(1, states)] for c in range(len(heights))]

    density = jnp.zeros((1, row_phi.shape[-1]), jnp.float32)
    for c in range(len(heights)):
        outgoing = pick(picks, parts[c, 0], arrived[c])
        gots = [outgoing[0]] + [swap(outgoing[d], "row", d) for d in range(1, owners)]
        density = contract(density, row_phi, col_phi, gots, sum(heights[:c]))
    return density.reshape(1, 1, 1, -1)


def solution(mesh):
    in_specs = (
        P("row", "state"),
        P("col", "state"),
        P("state"),
        P("state", "row", "col", None, None),
        P("state", "row", "col", None, None, None),
        P("state", "row", "col", None, None, None),
    )
    out_specs = P("state", "row", "col", None)
    return jax.shard_map(local, mesh=mesh, in_specs=in_specs, out_specs=out_specs, check_vma=False)
```

time: 81.2 us -> 28.6 us (0.35)
  blocking collectives: 72.1 us -> 0 us
  starting transfers between devices: 0 us -> 10.9 us
  Pallas kernels: 0 us -> 9.69 us
  matrix products: 8.25 us -> 0 us
  waiting for transfers between devices: 0 us -> 7.64 us
    psum x1 -> x0, blocking collectives: 54.9 us -> none  [local(): summed = lax.psum(partial_block, 'state')]
    all_to_all x1 -> x0, blocking collectives: 17.2 us -> none  [local(): lax.all_to_all(outgoing, 'row', split_axis=0, concat_axis=0, tiled=True)]
    ppermute x0 -> x12, starting transfers between devices: none -> 10.9 us  [swap(): lax.ppermute(value, axis, [(i, i ^ d) for i in range(lax.axis_size(axis))])]
    pallas_call x0 -> x8, Pallas kernels: none -> 9.69 us  [the longest x1 2.84 us: first(): pl.pallas_call(first_kernel, in_specs=[HBM] * 3, out_specs=VMEM, out_shap...]
    dot_general x3 -> x0, matrix products: 8.25 us -> none  [the longest x1 6.64 us: local(): lax.dot_general(weighted, coeff_cols, (((1,), (1,)), ((), ())), preferred...]
    ppermute x0 -> x12, waiting for transfers between devices: none -> 7.64 us  [swap(): lax.ppermute(value, axis, [(i, i ^ d) for i in range(lax.axis_size(axis))])]
  transfers between devices with their start and end apart: 0 -> 12, of which waited for: 0 -> 6; matrix products, arithmetic and copies ran while one was open for 0% -> 0% of each run, Pallas kernels for 0% -> 21%
where the time goes in v2:
time: 28.6 us; the launch traced here: 28.5 us
  starting transfers between devices  10.9 us (38%)
  Pallas kernels  9.69 us (34%)
  waiting for transfers between devices  7.64 us (27%)
    ppermute x12, starting transfers between devices, swap(): lax.ppermute(value, axis, [(i, i ^ d) for i in range(lax.axis_size(axis))])  10.9 us
    ppermute x12, waiting for transfers between devices, swap(): lax.ppermute(value, axis, [(i, i ^ d) for i in range(lax.axis_size(axis))])  7.64 us
    pallas_call x1, Pallas kernels, first(): pl.pallas_call(first_kernel, in_specs=[HBM] * 3, out_specs=VMEM, out_shap...  2.84 us
    pallas_call x1, Pallas kernels, rest(): pl.pallas_call(functools.partial(rest_kernel, heights), in_specs=[VMEM] *...  2.69 us
    pallas_call x3, Pallas kernels, pick(): pl.pallas_call(pick_kernel, in_specs=[SMEM] + [VMEM] * (1 + len(parts)),...  2.64 us
    pallas_call x3, Pallas kernels, contract(): pl.pallas_call(functools.partial(contract_kernel, start), in_specs=[VMEM]...  1.52 us
  transfers between devices with their start and end apart: 12, of which 6 were waited for; matrix products, arithmetic and copies ran while one was open for 0% of the time, Pallas kernels for 21%

profile of v2, /device:TPU:0, one launch (start us, length us, event | category | flops | bytes accessed | tf_op | source)
XLA Modules:
  0.0 28.5 jit_solution(17815236964760910418)
XLA Ops:
  0.0 2.8 %shard_map.65 = bf16[4,96,256]{2,1,0:T(8,128)(2,1)S(1)} custom-call(bf16[512,2048]{1,0:T(8,128)(2,1)} %rows_hbm.1, f32[1,2048]{1,0:T(1,128)} %bitcast.14, bf16[4,256,2048]{2,1,0:T(8,128)(2,1)} %bitcast.12), custom_call_target="tpu_custom_call" | custom-call | flops 402653184 | bytes 2621440 | tf_op jit(solution)/shard_map/pallas_call | solution.py:44
  2.9 3.0 %collective-permute-start = (bf16[4,96,256]{2,1,0:T(8,128)(2,1)S(1)}, bf16[4,96,256]{2,1,0:T(8,128)(2,1)}, u32[]{:S(2)}, u32[]{:S(2)}) collective-permute-start(bf16[4,96,256]{2,1,0:T(8,128)(2,1)S(1)} %shard_map.65), channel_id=1, source_target_pairs={{0,16},{16,0},{1,17},{17,1},{2,18},{18,2},{3,19},{19,3},{4,20},{20... | collective-permute-start | bytes 589832 | tf_op jit(solution)/shard_map/ppermute | solution.py:169
  5.9 2.7 %shard_map.64 = (f32[4,96,256]{2,1,0:T(8,128)S(1)}, f32[4,96,256]{2,1,0:T(8,128)S(1)}, bf16[4,96,256]{2,1,0:T(8,128)(2,1)}, f32[4,64,256]{2,1,0:T(8,128)S(1)}, bf16[4,64,256]{2,1,0:T(8,128)(2,1)}) custom-call(bf16[512,2048]{1,0:T(8,128)(2,1)S(1)} %copy-done.3, f32[1,2048]{1,0:T(1,128)S(1)} %bitcast.15, bf16[4,256,2048]{2,1,0:T(8,128)(2,1)S(1)} %bitcast.13), custom_call_target="tpu_custom_call" | custom-call | flops 2147483648 | bytes 6291456 | tf_op jit(solution)/shard_map/pallas_call | solution.py:89
  8.6 0.7 %collective-permute-start.4 = (bf16[4,96,256]{2,1,0:T(8,128)(2,1)}, bf16[4,96,256]{2,1,0:T(8,128)(2,1)S(1)}, u32[]{:S(2)}, u32[]{:S(2)}) collective-permute-start(bf16[4,96,256]{2,1,0:T(8,128)(2,1)} %get-tuple-element.28), channel_id=1, source_target_pairs={{0,16},{16,0},{1,17},{17,1},{2,18},{18,2},{3,19},{19,3},{4,20},{20... | collective-permute-start | bytes 589832 | tf_op jit(solution)/shard_map/ppermute | solution.py:169
  9.3 1.3 %collective-permute-start.8 = (bf16[4,64,256]{2,1,0:T(8,128)(2,1)}, bf16[4,64,256]{2,1,0:T(8,128)(2,1)}, u32[]{:S(2)}, u32[]{:S(2)}) collective-permute-start(bf16[4,64,256]{2,1,0:T(8,128)(2,1)} %get-tuple-element.34), channel_id=1, source_target_pairs={{0,16},{16,0},{1,17},{17,1},{2,18},{18,2},{3,19},{19,3},{4,20},{20... | collective-permute-start | bytes 393224 | tf_op jit(solution)/shard_map/ppermute | solution.py:169
  10.6 0.1 copy.7.picks_ref
  10.7 0.2 collective-permute-done.refs_0_
  10.9 1.0 %shard_map.66 = (bf16[2,96,256]{2,1,0:T(8,128)(2,1)S(1)}, bf16[2,96,256]{2,1,0:T(8,128)(2,1)S(1)}, bf16[2,96,256]{2,1,0:T(8,128)(2,1)S(1)}, bf16[2,96,256]{2,1,0:T(8,128)(2,1)S(1)}) custom-call(s32[4,2]{1,0:T(4,128)S(1)} %copy.7.picks_ref, f32[4,96,256]{2,1,0:T(8,128)S(1)} %get-tuple-element.22.own_ref, bf16[4,96,256]{2,1,0:T(8,128)(2,1)} %collective-permute-done.refs_0_), custom_call_target="tpu_custom_call" | custom-call | flops 98304 | bytes 786432 | tf_op jit(solution)/shard_map/pallas_call | solution.py:126
  12.0 1.9 %collective-permute-start.2 = (bf16[2,96,256]{2,1,0:T(8,128)(2,1)S(1)}, bf16[2,96,256]{2,1,0:T(8,128)(2,1)S(1)}, u32[]{:S(2)}, u32[]{:S(2)}) collective-permute-start(bf16[2,96,256]{2,1,0:T(8,128)(2,1)S(1)} %get-tuple-element.25), channel_id=1, source_target_pairs={{0,8},{4,12},{8,0},{12,4},{1,9},{5,13},{9,1},{13,5},{2,10},{6,14},... | collective-permute-start | bytes 294920 | tf_op jit(solution)/shard_map/ppermute | solution.py:169
  13.9 2.6 %collective-permute-done.4.refs_0_ = bf16[4,96,256]{2,1,0:T(8,128)(2,1)S(1)} collective-permute-done((bf16[4,96,256]{2,1,0:T(8,128)(2,1)}, bf16[4,96,256]{2,1,0:T(8,128)(2,1)S(1)}, u32[]{:S(2)}, u32[]{:S(2)}) %collective-permute-start.4) | collective-permute-done | bytes 196640 | tf_op jit(solution)/shard_map/ppermute | solution.py:169
  16.6 0.7 %shard_map.68 = (bf16[2,96,256]{2,1,0:T(8,128)(2,1)S(1)}, bf16[2,96,256]{2,1,0:T(8,128)(2,1)S(1)}, bf16[2,96,256]{2,1,0:T(8,128)(2,1)S(1)}, bf16[2,96,256]{2,1,0:T(8,128)(2,1)S(1)}) custom-call(s32[4,2]{1,0:T(4,128)S(1)} %copy.7.picks_ref, f32[4,96,256]{2,1,0:T(8,128)S(1)} %get-tuple-element.27.own_ref, bf16[4,96,256]{2,1,0:T(8,128)(2,1)S(1)} %collective-permute-done.4.refs_0_), custom_call_target="tpu_custom_call" | custom-call | flops 98304 | bytes 786432 | tf_op jit(solution)/shard_map/pallas_call | solution.py:126
  17.2 0.1 collective-permute-start.5
  17.3 0.8 %collective-permute-done.8.refs_0_ = bf16[4,64,256]{2,1,0:T(8,128)(2,1)} collective-permute-done((bf16[4,64,256]{2,1,0:T(8,128)(2,1)}, bf16[4,64,256]{2,1,0:T(8,128)(2,1)}, u32[]{:S(2)}, u32[]{:S(2)}) %collective-permute-start.8) | collective-permute-done | bytes 131104 | tf_op jit(solution)/shard_map/ppermute | solution.py:169
  18.1 1.6 %collective-permute-start.6 = (bf16[2,96,256]{2,1,0:T(8,128)(2,1)S(1)}, bf16[2,96,256]{2,1,0:T(8,128)(2,1)S(1)}, u32[]{:S(2)}, u32[]{:S(2)}) collective-permute-start(bf16[2,96,256]{2,1,0:T(8,128)(2,1)S(1)} %get-tuple-element.31), channel_id=1, source_target_pairs={{0,8},{4,12},{8,0},{12,4},{1,9},{5,13},{9,1},{13,5},{2,10},{6,14},... | collective-permute-start | bytes 294920 | tf_op jit(solution)/shard_map/ppermute | solution.py:169
  19.7 1.0 %shard_map.70 = (bf16[2,64,256]{2,1,0:T(8,128)(2,1)S(1)}, bf16[2,64,256]{2,1,0:T(8,128)(2,1)S(1)}, bf16[2,64,256]{2,1,0:T(8,128)(2,1)S(1)}, bf16[2,64,256]{2,1,0:T(8,128)(2,1)S(1)}) custom-call(s32[4,2]{1,0:T(4,128)S(1)} %copy.7.picks_ref, f32[4,64,256]{2,1,0:T(8,128)S(1)} %get-tuple-element.33.own_ref, bf16[4,64,256]{2,1,0:T(8,128)(2,1)} %collective-permute-done.8.refs_0_), custom_call_target="tpu_custom_call" | custom-call | flops 65536 | bytes 524288 | tf_op jit(solution)/shard_map/pallas_call | solution.py:126
  20.7 1.1 %collective-permute-start.10 = (bf16[2,64,256]{2,1,0:T(8,128)(2,1)S(1)}, bf16[2,64,256]{2,1,0:T(8,128)(2,1)S(1)}, u32[]{:S(2)}, u32[]{:S(2)}) collective-permute-start(bf16[2,64,256]{2,1,0:T(8,128)(2,1)S(1)} %get-tuple-element.37), channel_id=1, source_target_pairs={{0,8},{4,12},{8,0},{12,4},{1,9},{5,13},{9,1},{13,5},{2,10},{6,14},... | collective-permute-start | bytes 196616 | tf_op jit(solution)/shard_map/ppermute | solution.py:169
  21.8 0.8 %collective-permute-start.11 = (bf16[2,64,256]{2,1,0:T(8,128)(2,1)S(1)}, bf16[2,64,256]{2,1,0:T(8,128)(2,1)S(1)}, u32[]{:S(2)}, u32[]{:S(2)}) collective-permute-start(bf16[2,64,256]{2,1,0:T(8,128)(2,1)S(1)} %get-tuple-element.38), channel_id=1, source_target_pairs={{0,12},{4,8},{8,4},{12,0},{1,13},{5,9},{9,5},{13,1},{2,14},{6,10},... | collective-permute-start | bytes 196616 | tf_op jit(solution)/shard_map/ppermute | solution.py:169
  22.6 0.3 collective-permute-start.9
  22.9 0.3 %shard_map.67.before_ref = f32[1,256]{1,0:T(1,128)S(1)} custom-call(f32[1,256]{1,0:T(1,128)S(1)} %broadcast_in_dim.6.before_ref, bf16[8,256,256]{2,1,0:T(8,128)(2,1)S(1)} %bitcast.6, bf16[8,256,256]{2,1,0:T(8,128)(2,1)S(1)} %bitcast.9, bf16[2,96,256]{2,1,0:T(8,128)(2,1)S(1)} %get-tuple-element.23.refs_0_, ...), custom_call_target="tpu_custom_call" | custom-call | flops 100663296 | bytes 1048576 | tf_op jit(solution)/shard_map/pallas_call | solution.py:156
  23.2 1.5 %collective-permute-done.7.refs_3_ = bf16[2,96,256]{2,1,0:T(8,128)(2,1)S(1)} collective-permute-done((bf16[2,96,256]{2,1,0:T(8,128)(2,1)S(1)}, bf16[2,96,256]{2,1,0:T(8,128)(2,1)S(1)}, u32[]{:S(2)}, u32[]{:S(2)}) %collective-permute-start.7) | collective-permute-done | bytes 98336 | tf_op jit(solution)/shard_map/ppermute | solution.py:169
  24.8 0.3 %shard_map.69.before_ref = f32[1,256]{1,0:T(1,128)S(1)} custom-call(f32[1,256]{1,0:T(1,128)S(1)} %shard_map.67.before_ref, bf16[8,256,256]{2,1,0:T(8,128)(2,1)S(1)} %bitcast.7, bf16[8,256,256]{2,1,0:T(8,128)(2,1)S(1)} %bitcast.10, bf16[2,96,256]{2,1,0:T(8,128)(2,1)S(1)} %get-tuple-element.29.refs_0_, bf16[2,96,256]{2,1,0:T(8,128)(2,1)S(1)} %collective-permute-done.5.refs_1_, ...), custom_call_target="tpu_custom_call" | custom-call | flops 100663296 | bytes 1048576 | tf_op jit(solution)/shard_map/pallas_call | solution.py:156
  25.1 1.1 %collective-permute-done.10.refs_2_ = bf16[2,64,256]{2,1,0:T(8,128)(2,1)S(1)} collective-permute-done((bf16[2,64,256]{2,1,0:T(8,128)(2,1)S(1)}, bf16[2,64,256]{2,1,0:T(8,128)(2,1)S(1)}, u32[]{:S(2)}, u32[]{:S(2)}) %collective-permute-start.10) | collective-permute-done | bytes 65568 | tf_op jit(solution)/shard_map/ppermute | solution.py:169
  26.2 1.4 %collective-permute-done.11.refs_3_ = bf16[2,64,256]{2,1,0:T(8,128)(2,1)S(1)} collective-permute-done((bf16[2,64,256]{2,1,0:T(8,128)(2,1)S(1)}, bf16[2,64,256]{2,1,0:T(8,128)(2,1)S(1)}, u32[]{:S(2)}, u32[]{:S(2)}) %collective-permute-start.11) | collective-permute-done | bytes 65568 | tf_op jit(solution)/shard_map/ppermute | solution.py:169
  27.6 0.9 %shard_map.71 = f32[1,256]{1,0:T(1,128)} custom-call(f32[1,256]{1,0:T(1,128)S(1)} %shard_map.69.before_ref, bf16[8,256,256]{2,1,0:T(8,128)(2,1)S(1)} %bitcast.8, bf16[8,256,256]{2,1,0:T(8,128)(2,1)S(1)} %bitcast.11, bf16[2,64,256]{2,1,0:T(8,128)(2,1)S(1)} %get-tuple-element.35.refs_0_, bf16[2,64,256]{2,1,0:T(8,128)(2,1)S(1)} %collective-permute-done.9.refs_1_, ...), custom_call_target="tpu_custom_call" | custom-call | flops 67108864 | bytes 1048576 | tf_op jit(solution)/shard_map/pallas_call | solution.py:156
  (22 shorter events, 0.2 us)
Async XLA Ops:
  0.0 5.9 %copy-start.4 = (f32[2048]{0:T(1024)S(1)}, f32[2048]{0:T(1024)}, u32[]{:S(2)}) copy-start(f32[2048]{0:T(1024)} %param.8) | copy-start | bytes 24580
  0.0 5.9 %copy-start.2 = (bf16[1024,2048]{1,0:T(8,128)(2,1)S(1)}, bf16[1024,2048]{1,0:T(8,128)(2,1)}, u32[]{:S(2)}) copy-start(bf16[1024,2048]{1,0:T(8,128)(2,1)} %param.7) | copy-start | bytes 12582916
  0.0 5.9 %copy-start.3 = (bf16[512,2048]{1,0:T(8,128)(2,1)S(1)}, bf16[512,2048]{1,0:T(8,128)(2,1)}, u32[]{:S(2)}) copy-start(bf16[512,2048]{1,0:T(8,128)(2,1)} %rows_hbm.1) | copy-start | bytes 6291460
  2.9 7.8 %copy-start.5 = (s32[1,1,1,4,2]{3,4,2,1,0:T(2,128)S(1)}, s32[1,1,1,4,2]{3,4,2,1,0:T(2,128)}, u32[]{:S(2)}) copy-start(s32[1,1,1,4,2]{3,4,2,1,0:T(2,128)} %param.9) | copy-start | bytes 100
  2.9 20.0 %copy-start = (bf16[1,1,1,8,256,256]{5,4,3,2,1,0:T(8,128)(2,1)S(1)}, bf16[1,1,1,8,256,256]{5,4,3,2,1,0:T(8,128)(2,1)}, u32[]{:S(2)}) copy-start(bf16[1,1,1,8,256,256]{5,4,3,2,1,0:T(8,128)(2,1)} %param.10) | copy-start | bytes 3145732
  2.9 20.0 %copy-start.1 = (bf16[1,1,1,8,256,256]{5,4,3,2,1,0:T(8,128)(2,1)S(1)}, bf16[1,1,1,8,256,256]{5,4,3,2,1,0:T(8,128)(2,1)}, u32[]{:S(2)}) copy-start(bf16[1,1,1,8,256,256]{5,4,3,2,1,0:T(8,128)(2,1)} %param.11) | copy-start | bytes 3145732
  2.9 8.0 %collective-permute-start = (bf16[4,96,256]{2,1,0:T(8,128)(2,1)S(1)}, bf16[4,96,256]{2,1,0:T(8,128)(2,1)}, u32[]{:S(2)}, u32[]{:S(2)}) collective-permute-start(bf16[4,96,256]{2,1,0:T(8,128)(2,1)S(1)} %shard_map.65), channel_id=1, source_target_pairs={{0,16},{16,0},{1,17},{17,1},{2,18},{18,2},{3,19},{19,3},{4,20},{20... | collective-permute-start | bytes 589832 | tf_op jit(solution)/shard_map/ppermute | solution.py:169
  8.6 8.0 %collective-permute-start.4 = (bf16[4,96,256]{2,1,0:T(8,128)(2,1)}, bf16[4,96,256]{2,1,0:T(8,128)(2,1)S(1)}, u32[]{:S(2)}, u32[]{:S(2)}) collective-permute-start(bf16[4,96,256]{2,1,0:T(8,128)(2,1)} %get-tuple-element.28), channel_id=1, source_target_pairs={{0,16},{16,0},{1,17},{17,1},{2,18},{18,2},{3,19},{19,3},{4,20},{20... | collective-permute-start | bytes 589832 | tf_op jit(solution)/shard_map/ppermute | solution.py:169
  9.3 8.8 %collective-permute-start.8 = (bf16[4,64,256]{2,1,0:T(8,128)(2,1)}, bf16[4,64,256]{2,1,0:T(8,128)(2,1)}, u32[]{:S(2)}, u32[]{:S(2)}) collective-permute-start(bf16[4,64,256]{2,1,0:T(8,128)(2,1)} %get-tuple-element.34), channel_id=1, source_target_pairs={{0,16},{16,0},{1,17},{17,1},{2,18},{18,2},{3,19},{19,3},{4,20},{20... | collective-permute-start | bytes 393224 | tf_op jit(solution)/shard_map/ppermute | solution.py:169
  11.9 7.8 %collective-permute-start.1 = (bf16[2,96,256]{2,1,0:T(8,128)(2,1)S(1)}, bf16[2,96,256]{2,1,0:T(8,128)(2,1)S(1)}, u32[]{:S(2)}, u32[]{:S(2)}) collective-permute-start(bf16[2,96,256]{2,1,0:T(8,128)(2,1)S(1)} %get-tuple-element.24), channel_id=1, source_target_pairs={{0,4},{4,0},{8,12},{12,8},{1,5},{5,1},{9,13},{13,9},{2,6},{6,2},{1... | collective-permute-start | bytes 294920 | tf_op jit(solution)/shard_map/ppermute | solution.py:169
  12.0 8.7 %collective-permute-start.2 = (bf16[2,96,256]{2,1,0:T(8,128)(2,1)S(1)}, bf16[2,96,256]{2,1,0:T(8,128)(2,1)S(1)}, u32[]{:S(2)}, u32[]{:S(2)}) collective-permute-start(bf16[2,96,256]{2,1,0:T(8,128)(2,1)S(1)} %get-tuple-element.25), channel_id=1, source_target_pairs={{0,8},{4,12},{8,0},{12,4},{1,9},{5,13},{9,1},{13,5},{2,10},{6,14},... | collective-permute-start | bytes 294920 | tf_op jit(solution)/shard_map/ppermute | solution.py:169
  13.9 7.9 %collective-permute-start.3 = (bf16[2,96,256]{2,1,0:T(8,128)(2,1)S(1)}, bf16[2,96,256]{2,1,0:T(8,128)(2,1)S(1)}, u32[]{:S(2)}, u32[]{:S(2)}) collective-permute-start(bf16[2,96,256]{2,1,0:T(8,128)(2,1)S(1)} %get-tuple-element.26), channel_id=1, source_target_pairs={{0,12},{4,8},{8,4},{12,0},{1,13},{5,9},{9,5},{13,1},{2,14},{6,10},... | collective-permute-start | bytes 294920 | tf_op jit(solution)/shard_map/ppermute | solution.py:169
  17.2 5.4 %collective-permute-start.5 = (bf16[2,96,256]{2,1,0:T(8,128)(2,1)S(1)}, bf16[2,96,256]{2,1,0:T(8,128)(2,1)S(1)}, u32[]{:S(2)}, u32[]{:S(2)}) collective-permute-start(bf16[2,96,256]{2,1,0:T(8,128)(2,1)S(1)} %get-tuple-element.30), channel_id=1, source_target_pairs={{0,4},{4,0},{8,12},{12,8},{1,5},{5,1},{9,13},{13,9},{2,6},{6,2},{1... | collective-permute-start | bytes 294920 | tf_op jit(solution)/shard_map/ppermute | solution.py:169
  18.1 5.2 %collective-permute-start.6 = (bf16[2,96,256]{2,1,0:T(8,128)(2,1)S(1)}, bf16[2,96,256]{2,1,0:T(8,128)(2,1)S(1)}, u32[]{:S(2)}, u32[]{:S(2)}) collective-permute-start(bf16[2,96,256]{2,1,0:T(8,128)(2,1)S(1)} %get-tuple-element.31), channel_id=1, source_target_pairs={{0,8},{4,12},{8,0},{12,4},{1,9},{5,13},{9,1},{13,5},{2,10},{6,14},... | collective-permute-start | bytes 294920 | tf_op jit(solution)/shard_map/ppermute | solution.py:169
  19.7 5.1 %collective-permute-start.7 = (bf16[2,96,256]{2,1,0:T(8,128)(2,1)S(1)}, bf16[2,96,256]{2,1,0:T(8,128)(2,1)S(1)}, u32[]{:S(2)}, u32[]{:S(2)}) collective-permute-start(bf16[2,96,256]{2,1,0:T(8,128)(2,1)S(1)} %get-tuple-element.32), channel_id=1, source_target_pairs={{0,12},{4,8},{8,4},{12,0},{1,13},{5,9},{9,5},{13,1},{2,14},{6,10},... | collective-permute-start | bytes 294920 | tf_op jit(solution)/shard_map/ppermute | solution.py:169
  20.7 5.5 %collective-permute-start.10 = (bf16[2,64,256]{2,1,0:T(8,128)(2,1)S(1)}, bf16[2,64,256]{2,1,0:T(8,128)(2,1)S(1)}, u32[]{:S(2)}, u32[]{:S(2)}) collective-permute-start(bf16[2,64,256]{2,1,0:T(8,128)(2,1)S(1)} %get-tuple-element.37), channel_id=1, source_target_pairs={{0,8},{4,12},{8,0},{12,4},{1,9},{5,13},{9,1},{13,5},{2,10},{6,14},... | collective-permute-start | bytes 196616 | tf_op jit(solution)/shard_map/ppermute | solution.py:169
  21.8 5.8 %collective-permute-start.11 = (bf16[2,64,256]{2,1,0:T(8,128)(2,1)S(1)}, bf16[2,64,256]{2,1,0:T(8,128)(2,1)S(1)}, u32[]{:S(2)}, u32[]{:S(2)}) collective-permute-start(bf16[2,64,256]{2,1,0:T(8,128)(2,1)S(1)} %get-tuple-element.38), channel_id=1, source_target_pairs={{0,12},{4,8},{8,4},{12,0},{1,13},{5,9},{9,5},{13,1},{2,14},{6,10},... | collective-permute-start | bytes 196616 | tf_op jit(solution)/shard_map/ppermute | solution.py:169
  22.6 5.0 %collective-permute-start.9 = (bf16[2,64,256]{2,1,0:T(8,128)(2,1)S(1)}, bf16[2,64,256]{2,1,0:T(8,128)(2,1)S(1)}, u32[]{:S(2)}, u32[]{:S(2)}) collective-permute-start(bf16[2,64,256]{2,1,0:T(8,128)(2,1)S(1)} %get-tuple-element.36), channel_id=1, source_target_pairs={{0,4},{4,0},{8,12},{12,8},{1,5},{5,1},{9,13},{13,9},{2,6},{6,2},{1... | collective-permute-start | bytes 196616 | tf_op jit(solution)/shard_map/ppermute | solution.py:169

commit v3 on v2

--- a/solution.py
+++ b/solution.py
@@ -13,6 +13,9 @@
 VMEM = pl.BlockSpec(memory_space=pltpu.VMEM)
 SMEM = pl.BlockSpec(memory_space=pltpu.SMEM)
 HBM = pl.BlockSpec(memory_space=pltpu.HBM)
+ANY = pl.BlockSpec(memory_space=pl.ANY)
+NEAR = 2
+STEP_FLOPS = 3 * 10**9
 
 
 def params(mib):
@@ -63,7 +66,7 @@
     )(*(pltpu.with_memory_space_constraint(x, pltpu.HBM) for x in operands))
 
 
-def rest_kernel(heights, rows_ref, occ_ref, cols_ref, *refs):
+def rest_kernel(heights, rows_ref, occ_ref, cols_ref, _, *refs):
     outs, weighted_ref = list(refs[:-1]), refs[-1]
     groups, side = weighted_ref.shape[0] // cols_ref.shape[1], cols_ref.shape[1]
     states = weighted_ref.shape[1]
@@ -82,13 +85,13 @@
         start += height
 
 
-def rest(heights, coeff_rows, occupation, coeff_cols, side):
+def rest(heights, coeff_rows, occupation, coeff_cols, side, after):
     count, _, states = coeff_cols.shape
     groups = coeff_rows.shape[0] // side
     keys = [(c, d) for c in range(len(heights)) for d in range(groups) if (c, d) != (0, 1)]
     outs = pl.pallas_call(
         functools.partial(rest_kernel, heights),
-        in_specs=[VMEM] * 3,
+        in_specs=[VMEM] * 3 + [ANY],
         out_specs=[VMEM] * len(keys),
         out_shape=[
             jax.ShapeDtypeStruct((count, heights[c], side), jnp.bfloat16 if d else jnp.float32) for c, d in keys
@@ -100,48 +103,96 @@
             bytes_accessed=2 * states * (count + groups) * side,
             transcendentals=0,
         ),
-    )(coeff_rows, occupation, coeff_cols)
+    )(coeff_rows, occupation, coeff_cols, after)
     return dict(zip(keys, outs))
 
 
-def pick_kernel(picks_ref, own_ref, *refs):
-    tiles_ref = refs[-1]
+def spread_kernel(picks_ref, out):
     owners, slots = picks_ref.shape
     row = lax.axis_index("row")
-    parts, outs = refs[: -1 - owners], refs[-1 - owners : -1]
-    count = own_ref.shape[0]
-    total = own_ref[...]
-    for part in parts:
-        total = total + part[...].astype(jnp.float32)
-    tiles_ref[:count] = total.astype(jnp.bfloat16)
-    tiles_ref[count] = jnp.zeros(tiles_ref.shape[1:], jnp.bfloat16)
-    for d, out in enumerate(outs):
+    for d in range(owners):
         for k in range(slots):
-            out[k] = tiles_ref[picks_ref[row ^ d, k]]
-
-
-def pick(picks, own, parts):
+            out[d * slots + k] = jnp.full(out.shape[1:], picks_ref[row ^ d, k], jnp.int32)
+
+
+def spread(picks, side):
+    return pl.pallas_call(
+        spread_kernel,
+        in_specs=[SMEM],
+        out_specs=VMEM,
+        out_shape=jax.ShapeDtypeStruct((picks.size, 8, side), jnp.int32),
+        compiler_params=params(8),
+    )(picks)
+
+
+def listed_tile(listed, tiles):
+    chosen = jnp.zeros_like(tiles[0])
+    for t, tile in enumerate(tiles):
+        chosen = jnp.where(listed == t, tile, chosen)
+    return chosen.astype(jnp.bfloat16)
+
+
+def pick_kernel(groups, far, slots, lists_ref, own_ref, *refs):
+    parts, tiles_ref, outs = refs[: groups - 1], refs[-1 - far], refs[-far:]
+    tiles = []
+    for t in range(own_ref.shape[0]):
+        total = own_ref[t]
+        for part in parts:
+            total = total + part[t].astype(jnp.float32)
+        tiles.append(total)
+        tiles_ref[t] = total.astype(jnp.bfloat16)
+    for d, out in enumerate(outs, NEAR):
+        for k in range(slots):
+            out[k] = listed_tile(lists_ref[d * slots + k, :1], tiles)
+
+
+def pick(lists, slots, own, parts, after):
     count, height, side = own.shape
-    owners, slots = picks.shape
-    return pl.pallas_call(
-        pick_kernel,
-        in_specs=[SMEM] + [VMEM] * (1 + len(parts)),
-        out_specs=[VMEM] * owners,
-        out_shape=[jax.ShapeDtypeStruct((slots, height, side), jnp.bfloat16)] * owners,
-        scratch_shapes=[pltpu.VMEM((count + 1, height, side), jnp.bfloat16)],
-        compiler_params=params(8),
-        cost_estimate=pl.CostEstimate(
-            flops=count * height * side, bytes_accessed=8 * count * height * side, transcendentals=0
-        ),
-    )(picks, own, *parts)
-
-
-def contract_kernel(start, before_ref, row_phi_ref, col_phi_ref, *refs):
-    gots, out = refs[:-1], refs[-1]
+    owners = lists.shape[0] // slots
+    return pl.pallas_call(
+        functools.partial(pick_kernel, 1 + len(parts), owners - NEAR, slots),
+        in_specs=[VMEM] * (2 + len(parts)) + [ANY] * len(after),
+        out_specs=[VMEM] * (1 + owners - NEAR),
+        out_shape=[jax.ShapeDtypeStruct((count, height, side), jnp.bfloat16)]
+        + [jax.ShapeDtypeStruct((slots, height, side), jnp.bfloat16)] * (owners - NEAR),
+        compiler_params=params(8),
+        cost_estimate=pl.CostEstimate(
+            flops=STEP_FLOPS, bytes_accessed=count * height * side, transcendentals=0
+        ),
+    )(lists, own, *parts, *after)
+
+
+def near_kernel(slots, lists_ref, *refs):
+    chunks, outs = refs[:-NEAR], refs[-NEAR:]
+    start = 0
+    for chunk in chunks:
+        count, height, side = chunk.shape
+        tiles = [chunk[t].astype(jnp.float32) for t in range(count)]
+        for d, out in enumerate(outs):
+            for k in range(slots):
+                out[k, start : start + height] = listed_tile(lists_ref[d * slots + k, :1], tiles)
+        start += height
+
+
+def pick_near(lists, slots, chunks):
+    side = sum(chunk.shape[1] for chunk in chunks)
+    shape = jax.ShapeDtypeStruct((slots, side, chunks[0].shape[2]), jnp.bfloat16)
+    return pl.pallas_call(
+        functools.partial(near_kernel, slots),
+        in_specs=[VMEM] * (1 + len(chunks)),
+        out_specs=[VMEM] * NEAR,
+        out_shape=[shape] * NEAR,
+        compiler_params=params(8),
+        cost_estimate=pl.CostEstimate(flops=STEP_FLOPS, bytes_accessed=side * side, transcendentals=0),
+    )(lists, *chunks)
+
+
+def contract_kernel(base, count, start, before_ref, row_phi_ref, col_phi_ref, *refs):
+    gots, out = refs[:count], refs[-1]
     row = lax.axis_index("row")
     cut = pl.ds(start, gots[0].shape[1])
     density = before_ref[...]
-    for d, got in enumerate(gots):
+    for d, got in enumerate(gots, base):
         slots = got.shape[0]
         for k in range(slots):
             m = (row ^ d) * slots + k
@@ -150,19 +201,21 @@
     out[...] = density
 
 
-def contract(before, row_phi, col_phi, gots, start):
+def contract(before, row_phi, col_phi, gots, base, start, after=()):
     received, side, points = col_phi.shape
-    height = gots[0].shape[1]
-    return pl.pallas_call(
-        functools.partial(contract_kernel, start),
-        in_specs=[VMEM] * (3 + len(gots)),
+    slots, height, _ = gots[0].shape
+    return pl.pallas_call(
+        functools.partial(contract_kernel, base, len(gots), start),
+        in_specs=[VMEM] * (3 + len(gots)) + [ANY] * len(after),
         out_specs=VMEM,
         out_shape=jax.ShapeDtypeStruct((1, points), jnp.float32),
         compiler_params=params(8),
         cost_estimate=pl.CostEstimate(
-            flops=2 * received * height * side * points, bytes_accessed=2 * received * side * points, transcendentals=0
-        ),
-    )(before, row_phi, col_phi, *gots)
+            flops=STEP_FLOPS,
+            bytes_accessed=received * side * points,
+            transcendentals=0,
+        ),
+    )(before, row_phi, col_phi, *gots, *after)
 
 
 def swap(value, axis, d):
@@ -171,21 +224,33 @@
 
 def local(coeff_rows, coeff_cols, occupation, send_list, row_phi, col_phi):
     states, owners = lax.axis_size("state"), lax.axis_size("row")
-    side = coeff_rows.shape[0] // states
+    side, slots = coeff_rows.shape[0] // states, send_list.shape[-1]
     heights = [side * n // 8 for n in EIGHTHS]
     row_phi, col_phi, picks = row_phi[0, 0, 0], col_phi[0, 0, 0], send_list[0, 0, 0]
     factors = coeff_rows, occupation[None, :], coeff_cols.reshape(-1, side, coeff_cols.shape[1]), side
 
+    lists = spread(picks, side)
     early = first(heights[0], *factors)
-    parts = rest(heights, *factors)
+    parts = rest(heights, *factors, early)
     parts[0, 1] = early
+
     arrived = [[swap(parts[c, d], "state", d) for d in range(1, states)] for c in range(len(heights))]
 
+    starts = [sum(heights[:c]) for c in range(len(heights))]
+    tiles, far, after = [], [], []
     density = jnp.zeros((1, row_phi.shape[-1]), jnp.float32)
     for c in range(len(heights)):
-        outgoing = pick(picks, parts[c, 0], arrived[c])
-        gots = [outgoing[0]] + [swap(outgoing[d], "row", d) for d in range(1, owners)]
-        density = contract(density, row_phi, col_phi, gots, sum(heights[:c]))
+        chunk, *outgoing = pick(lists, slots, parts[c, 0], arrived[c], after)
+        tiles.append(chunk)
+        after = [chunk]
+        far.append([swap(out, "row", d) for d, out in enumerate(outgoing, NEAR)])
+        if 1 <= c < len(heights) - 1:
+            density = contract(density, row_phi, col_phi, far[c - 1], NEAR, starts[c - 1], after)
+            after = [density]
+    mine, other = pick_near(lists, slots, tiles)
+    density = contract(density, row_phi, col_phi, far[-2], NEAR, starts[-2], [mine])
+    density = contract(density, row_phi, col_phi, [mine, swap(other, "row", 1)], 0, 0)
+    density = contract(density, row_phi, col_phi, far[-1], NEAR, starts[-1])
     return density.reshape(1, 1, 1, -1)
 
 

time: 28.6 us -> 26.5 us (0.927)
  Pallas kernels: 9.69 us -> 7.58 us
  starting transfers between devices: 10.9 us -> 11.4 us
  waiting for transfers between devices: 7.64 us -> 7.18 us
    pallas_call x6 -> x9, Pallas kernels: 4.15 us -> 2.73 us  [the longest x4 1.6 us: contract(): pl.pallas_call(functools.partial(contract_kernel, base, len(gots), start)...]
    pallas_call x1, Pallas kernels: 2.69 us -> 2.01 us  [rest(): pl.pallas_call(functools.partial(rest_kernel, heights), in_specs=[VMEM] *...]
    ppermute x12 -> x10, starting transfers between devices: 10.9 us -> 11.4 us  [swap(): lax.ppermute(value, axis, [(i, i ^ d) for i in range(lax.axis_size(axis))])]
    ppermute x12 -> x10, waiting for transfers between devices: 7.64 us -> 7.18 us  [swap(): lax.ppermute(value, axis, [(i, i ^ d) for i in range(lax.axis_size(axis))])]
  transfers between devices with their start and end apart: 12 -> 10, of which waited for: 6 -> 6; matrix products, arithmetic and copies ran while one was open for 0% -> 0% of each run, Pallas kernels for 21% -> 15%
where the time goes in v3:
time: 26.5 us; the launch traced here: 26.4 us
  starting transfers between devices  11.4 us (43%)
  Pallas kernels  7.58 us (29%)
  waiting for transfers between devices  7.18 us (27%)
    ppermute x10, starting transfers between devices, swap(): lax.ppermute(value, axis, [(i, i ^ d) for i in range(lax.axis_size(axis))])  11.4 us
    ppermute x10, waiting for transfers between devices, swap(): lax.ppermute(value, axis, [(i, i ^ d) for i in range(lax.axis_size(axis))])  7.18 us
    pallas_call x1, Pallas kernels, first(): pl.pallas_call(first_kernel, in_specs=[HBM] * 3, out_specs=VMEM, out_shap...  2.84 us
    pallas_call x1, Pallas kernels, rest(): pl.pallas_call(functools.partial(rest_kernel, heights), in_specs=[VMEM] *...  2.01 us
    pallas_call x4, Pallas kernels, contract(): pl.pallas_call(functools.partial(contract_kernel, base, len(gots), start)...  1.6 us
    pallas_call x1, Pallas kernels, spread(): pl.pallas_call(spread_kernel, in_specs=[SMEM], out_specs=VMEM, out_shape=...  0.58 us
  transfers between devices with their start and end apart: 10, of which 6 were waited for; matrix products, arithmetic and copies ran while one was open for 0% of the time, Pallas kernels for 15%

profile of v3, /device:TPU:0, one launch (start us, length us, event | category | flops | bytes accessed | tf_op | source)
XLA Modules:
  0.0 26.4 jit_solution(6777454027429732272)
XLA Ops:
  0.0 2.8 %shard_map.65._ = bf16[4,96,256]{2,1,0:T(8,128)(2,1)S(1)} custom-call(bf16[512,2048]{1,0:T(8,128)(2,1)} %rows_ref.1, f32[1,2048]{1,0:T(1,128)} %bitcast.8, bf16[4,256,2048]{2,1,0:T(8,128)(2,1)} %bitcast.6), custom_call_target="tpu_custom_call" | custom-call | flops 402653184 | bytes 2621440 | tf_op jit(solution)/shard_map/pallas_call | solution.py:47
  2.9 3.0 %collective-permute-start = (bf16[4,96,256]{2,1,0:T(8,128)(2,1)S(1)}, bf16[4,96,256]{2,1,0:T(8,128)(2,1)S(1)}, u32[]{:S(2)}, u32[]{:S(2)}) collective-permute-start(bf16[4,96,256]{2,1,0:T(8,128)(2,1)S(1)} %shard_map.65._), channel_id=1, source_target_pairs={{0,16},{16,0},{1,17},{17,1},{2,18},{18,2},{3,19},{19,3},{4,20},{20... | collective-permute-start | bytes 589832 | tf_op jit(solution)/shard_map/ppermute | solution.py:222
  5.9 2.0 %shard_map.66 = (f32[4,96,256]{2,1,0:T(8,128)S(1)}, f32[4,96,256]{2,1,0:T(8,128)S(1)}, bf16[4,96,256]{2,1,0:T(8,128)(2,1)S(1)}, f32[4,64,256]{2,1,0:T(8,128)S(1)}, bf16[4,64,256]{2,1,0:T(8,128)(2,1)S(1)}) custom-call(bf16[512,2048]{1,0:T(8,128)(2,1)S(1)} %copy-done.1, f32[1,2048]{1,0:T(1,128)S(1)} %bitcast.9, bf16[4,256,2048]{2,1,0:T(8,128)(2,1)S(1)} %bitcast.7, ...), custom_call_target="tpu_custom_call" | custom-call | flops 2147483648 | bytes 6291456 | tf_op jit(solution)/shard_map/pallas_call | solution.py:92
  7.9 0.8 %collective-permute-start.3 = (bf16[4,96,256]{2,1,0:T(8,128)(2,1)S(1)}, bf16[4,96,256]{2,1,0:T(8,128)(2,1)S(1)}, u32[]{:S(2)}, u32[]{:S(2)}) collective-permute-start(bf16[4,96,256]{2,1,0:T(8,128)(2,1)S(1)} %get-tuple-element.25), channel_id=1, source_target_pairs={{0,16},{16,0},{1,17},{17,1},{2,18},{18,2},{3,19},{19,3},{4,20},{20... | collective-permute-start | bytes 589832 | tf_op jit(solution)/shard_map/ppermute | solution.py:222
  8.7 1.3 %collective-permute-start.6 = (bf16[4,64,256]{2,1,0:T(8,128)(2,1)S(1)}, bf16[4,64,256]{2,1,0:T(8,128)(2,1)S(1)}, u32[]{:S(2)}, u32[]{:S(2)}) collective-permute-start(bf16[4,64,256]{2,1,0:T(8,128)(2,1)S(1)} %get-tuple-element.31), channel_id=1, source_target_pairs={{0,16},{16,0},{1,17},{17,1},{2,18},{18,2},{3,19},{19,3},{4,20},{20... | collective-permute-start | bytes 393224 | tf_op jit(solution)/shard_map/ppermute | solution.py:222
  10.0 0.1 copy.7.picks_ref
  10.1 0.6 %shard_map.64.lists_ref = s32[8,8,256]{2,1,0:T(8,128)S(1)} custom-call(s32[4,2]{1,0:T(4,128)S(1)} %copy.7.picks_ref), custom_call_target="tpu_custom_call" | custom-call | tf_op jit(solution)/shard_map/pallas_call | solution.py:119
  10.7 0.7 %collective-permute-done.refs_0_ = bf16[4,96,256]{2,1,0:T(8,128)(2,1)S(1)} collective-permute-done((bf16[4,96,256]{2,1,0:T(8,128)(2,1)S(1)}, bf16[4,96,256]{2,1,0:T(8,128)(2,1)S(1)}, u32[]{:S(2)}, u32[]{:S(2)}) %collective-permute-start) | collective-permute-done | bytes 196640 | tf_op jit(solution)/shard_map/ppermute | solution.py:222
  11.4 0.1 shard_map.67
  11.5 2.1 %collective-permute-start.1 = (bf16[2,96,256]{2,1,0:T(8,128)(2,1)S(1)}, bf16[2,96,256]{2,1,0:T(8,128)(2,1)S(1)}, u32[]{:S(2)}, u32[]{:S(2)}) collective-permute-start(bf16[2,96,256]{2,1,0:T(8,128)(2,1)S(1)} %get-tuple-element.22), channel_id=1, source_target_pairs={{0,8},{4,12},{8,0},{12,4},{1,9},{5,13},{9,1},{13,5},{2,10},{6,14},... | collective-permute-start | bytes 294920 | tf_op jit(solution)/shard_map/ppermute | solution.py:222
  13.6 2.2 %collective-permute-done.3.refs_0_ = bf16[4,96,256]{2,1,0:T(8,128)(2,1)S(1)} collective-permute-done((bf16[4,96,256]{2,1,0:T(8,128)(2,1)S(1)}, bf16[4,96,256]{2,1,0:T(8,128)(2,1)S(1)}, u32[]{:S(2)}, u32[]{:S(2)}) %collective-permute-start.3) | collective-permute-done | bytes 196640 | tf_op jit(solution)/shard_map/ppermute | solution.py:222
  15.8 0.1 shard_map.68
  15.9 1.9 %collective-permute-start.4 = (bf16[2,96,256]{2,1,0:T(8,128)(2,1)S(1)}, bf16[2,96,256]{2,1,0:T(8,128)(2,1)S(1)}, u32[]{:S(2)}, u32[]{:S(2)}) collective-permute-start(bf16[2,96,256]{2,1,0:T(8,128)(2,1)S(1)} %get-tuple-element.28), channel_id=1, source_target_pairs={{0,8},{4,12},{8,0},{12,4},{1,9},{5,13},{9,1},{13,5},{2,10},{6,14},... | collective-permute-start | bytes 294920 | tf_op jit(solution)/shard_map/ppermute | solution.py:222
  17.8 0.5 %collective-permute-done.2.refs_1_ = bf16[2,96,256]{2,1,0:T(8,128)(2,1)S(1)} collective-permute-done((bf16[2,96,256]{2,1,0:T(8,128)(2,1)S(1)}, bf16[2,96,256]{2,1,0:T(8,128)(2,1)S(1)}, u32[]{:S(2)}, u32[]{:S(2)}) %collective-permute-start.2) | collective-permute-done | bytes 98336 | tf_op jit(solution)/shard_map/ppermute | solution.py:222
  18.3 0.2 shard_map.69.refs_1_.before_ref
  18.5 0.1 shard_map.70
  18.6 0.2 shard_map.71
  18.9 2.3 %collective-permute-start.8 = (bf16[2,64,256]{2,1,0:T(8,128)(2,1)S(1)}, bf16[2,64,256]{2,1,0:T(8,128)(2,1)S(1)}, u32[]{:S(2)}, u32[]{:S(2)}) collective-permute-start(bf16[2,64,256]{2,1,0:T(8,128)(2,1)S(1)} %get-tuple-element.35), channel_id=1, source_target_pairs={{0,8},{4,12},{8,0},{12,4},{1,9},{5,13},{9,1},{13,5},{2,10},{6,14},... | collective-permute-start | bytes 196616 | tf_op jit(solution)/shard_map/ppermute | solution.py:222
  21.2 1.5 %collective-permute-done.5.refs_1_ = bf16[2,96,256]{2,1,0:T(8,128)(2,1)S(1)} collective-permute-done((bf16[2,96,256]{2,1,0:T(8,128)(2,1)S(1)}, bf16[2,96,256]{2,1,0:T(8,128)(2,1)S(1)}, u32[]{:S(2)}, u32[]{:S(2)}) %collective-permute-start.5) | collective-permute-done | bytes 98336 | tf_op jit(solution)/shard_map/ppermute | solution.py:222
  22.7 0.2 shard_map.72.before_ref
  22.9 0.3 %shard_map.73.before_ref = f32[1,256]{1,0:T(1,128)S(1)} custom-call(f32[1,256]{1,0:T(1,128)S(1)} %shard_map.72.before_ref, bf16[8,256,256]{2,1,0:T(8,128)(2,1)S(1)} %bitcast.12, bf16[8,256,256]{2,1,0:T(8,128)(2,1)S(1)} %bitcast.16, bf16[2,256,256]{2,1,0:T(8,128)(2,1)S(1)} %get-tuple-element.33.refs_2_.refs_0_, ...), custom_call_target="tpu_custom_call" | custom-call | flops 3000000000 | bytes 524288 | tf_op jit(solution)/shard_map/pallas_call | solution.py:207
  23.3 0.8 %collective-permute-done.8.refs_0_ = bf16[2,64,256]{2,1,0:T(8,128)(2,1)S(1)} collective-permute-done((bf16[2,64,256]{2,1,0:T(8,128)(2,1)S(1)}, bf16[2,64,256]{2,1,0:T(8,128)(2,1)S(1)}, u32[]{:S(2)}, u32[]{:S(2)}) %collective-permute-start.8) | collective-permute-done | bytes 65568 | tf_op jit(solution)/shard_map/ppermute | solution.py:222
  24.1 1.5 %collective-permute-done.9.refs_1_ = bf16[2,64,256]{2,1,0:T(8,128)(2,1)S(1)} collective-permute-done((bf16[2,64,256]{2,1,0:T(8,128)(2,1)S(1)}, bf16[2,64,256]{2,1,0:T(8,128)(2,1)S(1)}, u32[]{:S(2)}, u32[]{:S(2)}) %collective-permute-start.9) | collective-permute-done | bytes 65568 | tf_op jit(solution)/shard_map/ppermute | solution.py:222
  25.6 0.8 %shard_map.74 = f32[1,256]{1,0:T(1,128)} custom-call(f32[1,256]{1,0:T(1,128)S(1)} %shard_map.73.before_ref, bf16[8,256,256]{2,1,0:T(8,128)(2,1)S(1)} %bitcast.13, bf16[8,256,256]{2,1,0:T(8,128)(2,1)S(1)} %bitcast.17, bf16[2,64,256]{2,1,0:T(8,128)(2,1)S(1)} %collective-permute-done.8.refs_0_, bf16[2,64,256]{2,1,0:T(8,128)(2,1)S(1)} %collective-permute-done.9.refs_1_), custom_call_target="tpu_custom_call" | custom-call | flops 3000000000 | bytes 524288 | tf_op jit(solution)/shard_map/pallas_call | solution.py:207
  (21 shorter events, 0.1 us)
Async XLA Ops:
  0.0 5.9 %copy-start.2 = (f32[2048]{0:T(1024)S(1)}, f32[2048]{0:T(1024)}, u32[]{:S(2)}) copy-start(f32[2048]{0:T(1024)} %param.8) | copy-start | bytes 24580
  0.0 5.9 %copy-start = (bf16[1024,2048]{1,0:T(8,128)(2,1)S(1)}, bf16[1024,2048]{1,0:T(8,128)(2,1)}, u32[]{:S(2)}) copy-start(bf16[1024,2048]{1,0:T(8,128)(2,1)} %param.7) | copy-start | bytes 12582916
  0.0 5.9 %copy-start.1 = (bf16[512,2048]{1,0:T(8,128)(2,1)S(1)}, bf16[512,2048]{1,0:T(8,128)(2,1)}, u32[]{:S(2)}) copy-start(bf16[512,2048]{1,0:T(8,128)(2,1)} %rows_ref.1) | copy-start | bytes 6291460
  2.9 7.1 %copy-start.5 = (s32[1,1,1,4,2]{3,4,2,1,0:T(2,128)S(1)}, s32[1,1,1,4,2]{3,4,2,1,0:T(2,128)}, u32[]{:S(2)}) copy-start(s32[1,1,1,4,2]{3,4,2,1,0:T(2,128)} %param.9) | copy-start | bytes 100
  2.9 8.5 %collective-permute-start = (bf16[4,96,256]{2,1,0:T(8,128)(2,1)S(1)}, bf16[4,96,256]{2,1,0:T(8,128)(2,1)S(1)}, u32[]{:S(2)}, u32[]{:S(2)}) collective-permute-start(bf16[4,96,256]{2,1,0:T(8,128)(2,1)S(1)} %shard_map.65._), channel_id=1, source_target_pairs={{0,16},{16,0},{1,17},{17,1},{2,18},{18,2},{3,19},{19,3},{4,20},{20... | collective-permute-start | bytes 589832 | tf_op jit(solution)/shard_map/ppermute | solution.py:222
  7.9 7.9 %collective-permute-start.3 = (bf16[4,96,256]{2,1,0:T(8,128)(2,1)S(1)}, bf16[4,96,256]{2,1,0:T(8,128)(2,1)S(1)}, u32[]{:S(2)}, u32[]{:S(2)}) collective-permute-start(bf16[4,96,256]{2,1,0:T(8,128)(2,1)S(1)} %get-tuple-element.25), channel_id=1, source_target_pairs={{0,16},{16,0},{1,17},{17,1},{2,18},{18,2},{3,19},{19,3},{4,20},{20... | collective-permute-start | bytes 589832 | tf_op jit(solution)/shard_map/ppermute | solution.py:222
  8.7 9.8 %collective-permute-start.6 = (bf16[4,64,256]{2,1,0:T(8,128)(2,1)S(1)}, bf16[4,64,256]{2,1,0:T(8,128)(2,1)S(1)}, u32[]{:S(2)}, u32[]{:S(2)}) collective-permute-start(bf16[4,64,256]{2,1,0:T(8,128)(2,1)S(1)} %get-tuple-element.31), channel_id=1, source_target_pairs={{0,16},{16,0},{1,17},{17,1},{2,18},{18,2},{3,19},{19,3},{4,20},{20... | collective-permute-start | bytes 393224 | tf_op jit(solution)/shard_map/ppermute | solution.py:222
  11.5 6.3 %collective-permute-start.1 = (bf16[2,96,256]{2,1,0:T(8,128)(2,1)S(1)}, bf16[2,96,256]{2,1,0:T(8,128)(2,1)S(1)}, u32[]{:S(2)}, u32[]{:S(2)}) collective-permute-start(bf16[2,96,256]{2,1,0:T(8,128)(2,1)S(1)} %get-tuple-element.22), channel_id=1, source_target_pairs={{0,8},{4,12},{8,0},{12,4},{1,9},{5,13},{9,1},{13,5},{2,10},{6,14},... | collective-permute-start | bytes 294920 | tf_op jit(solution)/shard_map/ppermute | solution.py:222
  13.6 4.7 %collective-permute-start.2 = (bf16[2,96,256]{2,1,0:T(8,128)(2,1)S(1)}, bf16[2,96,256]{2,1,0:T(8,128)(2,1)S(1)}, u32[]{:S(2)}, u32[]{:S(2)}) collective-permute-start(bf16[2,96,256]{2,1,0:T(8,128)(2,1)S(1)} %get-tuple-element.23), channel_id=1, source_target_pairs={{0,12},{4,8},{8,4},{12,0},{1,13},{5,9},{9,5},{13,1},{2,14},{6,10},... | collective-permute-start | bytes 294920 | tf_op jit(solution)/shard_map/ppermute | solution.py:222
  15.8 2.5 %copy-start.3 = (bf16[1,1,1,8,256,256]{5,4,3,2,1,0:T(8,128)(2,1)S(1)}, bf16[1,1,1,8,256,256]{5,4,3,2,1,0:T(8,128)(2,1)}, u32[]{:S(2)}) copy-start(bf16[1,1,1,8,256,256]{5,4,3,2,1,0:T(8,128)(2,1)} %param.10) | copy-start | bytes 3145732
  15.8 2.5 %copy-start.4 = (bf16[1,1,1,8,256,256]{5,4,3,2,1,0:T(8,128)(2,1)S(1)}, bf16[1,1,1,8,256,256]{5,4,3,2,1,0:T(8,128)(2,1)}, u32[]{:S(2)}) copy-start(bf16[1,1,1,8,256,256]{5,4,3,2,1,0:T(8,128)(2,1)} %param.11) | copy-start | bytes 3145732
  15.9 5.3 %collective-permute-start.4 = (bf16[2,96,256]{2,1,0:T(8,128)(2,1)S(1)}, bf16[2,96,256]{2,1,0:T(8,128)(2,1)S(1)}, u32[]{:S(2)}, u32[]{:S(2)}) collective-permute-start(bf16[2,96,256]{2,1,0:T(8,128)(2,1)S(1)} %get-tuple-element.28), channel_id=1, source_target_pairs={{0,8},{4,12},{8,0},{12,4},{1,9},{5,13},{9,1},{13,5},{2,10},{6,14},... | collective-permute-start | bytes 294920 | tf_op jit(solution)/shard_map/ppermute | solution.py:222
  17.8 4.9 %collective-permute-start.5 = (bf16[2,96,256]{2,1,0:T(8,128)(2,1)S(1)}, bf16[2,96,256]{2,1,0:T(8,128)(2,1)S(1)}, u32[]{:S(2)}, u32[]{:S(2)}) collective-permute-start(bf16[2,96,256]{2,1,0:T(8,128)(2,1)S(1)} %get-tuple-element.29), channel_id=1, source_target_pairs={{0,12},{4,8},{8,4},{12,0},{1,13},{5,9},{9,5},{13,1},{2,14},{6,10},... | collective-permute-start | bytes 294920 | tf_op jit(solution)/shard_map/ppermute | solution.py:222
  18.9 4.1 %collective-permute-start.7 = (bf16[2,256,256]{2,1,0:T(8,128)(2,1)S(1)}, bf16[2,256,256]{2,1,0:T(8,128)(2,1)S(1)}, u32[]{:S(2)}, u32[]{:S(2)}) collective-permute-start(bf16[2,256,256]{2,1,0:T(8,128)(2,1)S(1)} %get-tuple-element.34), channel_id=1, source_target_pairs={{0,4},{4,0},{8,12},{12,8},{1,5},{5,1},{9,13},{13,9},{2,6},{6,2},{1... | collective-permute-start | bytes 786440 | tf_op jit(solution)/shard_map/ppermute | solution.py:222
  18.9 5.1 %collective-permute-start.8 = (bf16[2,64,256]{2,1,0:T(8,128)(2,1)S(1)}, bf16[2,64,256]{2,1,0:T(8,128)(2,1)S(1)}, u32[]{:S(2)}, u32[]{:S(2)}) collective-permute-start(bf16[2,64,256]{2,1,0:T(8,128)(2,1)S(1)} %get-tuple-element.35), channel_id=1, source_target_pairs={{0,8},{4,12},{8,0},{12,4},{1,9},{5,13},{9,1},{13,5},{2,10},{6,14},... | collective-permute-start | bytes 196616 | tf_op jit(solution)/shard_map/ppermute | solution.py:222
  21.2 4.4 %collective-permute-start.9 = (bf16[2,64,256]{2,1,0:T(8,128)(2,1)S(1)}, bf16[2,64,256]{2,1,0:T(8,128)(2,1)S(1)}, u32[]{:S(2)}, u32[]{:S(2)}) collective-permute-start(bf16[2,64,256]{2,1,0:T(8,128)(2,1)S(1)} %get-tuple-element.36), channel_id=1, source_target_pairs={{0,12},{4,8},{8,4},{12,0},{1,13},{5,9},{9,5},{13,1},{2,14},{6,10},... | collective-permute-start | bytes 196616 | tf_op jit(solution)/shard_map/ppermute | solution.py:222

commit v4 on v3

--- a/solution.py
+++ b/solution.py
@@ -7,7 +7,7 @@
 from jax.experimental.pallas import tpu as pltpu
 from jax.sharding import PartitionSpec as P
 
-EIGHTHS = (3, 3, 2)
+PARTS = (5, 7, 4)
 MIB = 1024 * 1024
 NT = (((1,), (1,)), ((), ()))
 VMEM = pl.BlockSpec(memory_space=pltpu.VMEM)
@@ -15,6 +15,7 @@
 HBM = pl.BlockSpec(memory_space=pltpu.HBM)
 ANY = pl.BlockSpec(memory_space=pl.ANY)
 NEAR = 2
+AHEAD = 2
 STEP_FLOPS = 3 * 10**9
 
 
@@ -225,7 +226,8 @@
 def local(coeff_rows, coeff_cols, occupation, send_list, row_phi, col_phi):
     states, owners = lax.axis_size("state"), lax.axis_size("row")
     side, slots = coeff_rows.shape[0] // states, send_list.shape[-1]
-    heights = [side * n // 8 for n in EIGHTHS]
+    bounds = [side * sum(PARTS[:n]) // sum(PARTS) // 16 * 16 for n in range(len(PARTS) + 1)]
+    heights = [after - before for before, after in zip(bounds, bounds[1:])]
     row_phi, col_phi, picks = row_phi[0, 0, 0], col_phi[0, 0, 0], send_list[0, 0, 0]
     factors = coeff_rows, occupation[None, :], coeff_cols.reshape(-1, side, coeff_cols.shape[1]), side
 
@@ -234,8 +236,10 @@
     parts = rest(heights, *factors, early)
     parts[0, 1] = early
 
-    arrived = [[swap(parts[c, d], "state", d) for d in range(1, states)] for c in range(len(heights))]
-
+    def send(c):
+        return [swap(parts[c, d], "state", d) for d in range(1, states)]
+
+    arrived = [send(c) for c in range(min(AHEAD, len(heights)))]
     starts = [sum(heights[:c]) for c in range(len(heights))]
     tiles, far, after = [], [], []
     density = jnp.zeros((1, row_phi.shape[-1]), jnp.float32)
@@ -244,6 +248,10 @@
         tiles.append(chunk)
         after = [chunk]
         far.append([swap(out, "row", d) for d, out in enumerate(outgoing, NEAR)])
+        if c + AHEAD < len(heights):
+            for d in range(1, states):
+                parts[c + AHEAD, d], _ = lax.optimization_barrier((parts[c + AHEAD, d], chunk))
+            arrived.append(send(c + AHEAD))
         if 1 <= c < len(heights) - 1:
             density = contract(density, row_phi, col_phi, far[c - 1], NEAR, starts[c - 1], after)
             after = [density]

time: 26.5 us -> 26 us (0.981)
  waiting for transfers between devices: 7.18 us -> 6.75 us
    ppermute x10, waiting for transfers between devices: 7.18 us -> 6.75 us  [swap(): lax.ppermute(value, axis, [(i, i ^ d) for i in range(lax.axis_size(axis))])]
where the time goes in v4:
time: 26 us; the launch traced here: 25.9 us
  starting transfers between devices  11.4 us (44%)
  Pallas kernels  7.48 us (29%)
  waiting for transfers between devices  6.75 us (26%)
    ppermute x10, starting transfers between devices, swap(): lax.ppermute(value, axis, [(i, i ^ d) for i in range(lax.axis_size(axis))])  11.4 us
    ppermute x10, waiting for transfers between devices, swap(): lax.ppermute(value, axis, [(i, i ^ d) for i in range(lax.axis_size(axis))])  6.75 us
    pallas_call x1, Pallas kernels, first(): pl.pallas_call(first_kernel, in_specs=[HBM] * 3, out_specs=VMEM, out_shap...  2.69 us
    pallas_call x1, Pallas kernels, rest(): pl.pallas_call(functools.partial(rest_kernel, heights), in_specs=[VMEM] *...  2.07 us
    pallas_call x4, Pallas kernels, contract(): pl.pallas_call(functools.partial(contract_kernel, base, len(gots), start)...  1.6 us
    pallas_call x1, Pallas kernels, spread(): pl.pallas_call(spread_kernel, in_specs=[SMEM], out_specs=VMEM, out_shape=...  0.58 us
  transfers between devices with their start and end apart: 10, of which 6 were waited for; matrix products, arithmetic and copies ran while one was open for 0% of the time, Pallas kernels for 15%

profile of v4, /device:TPU:0, one launch (start us, length us, event | category | flops | bytes accessed | tf_op | source)
XLA Modules:
  0.0 25.9 jit_solution(8498294106309067554)
XLA Ops:
  0.0 2.7 %shard_map.65._ = bf16[4,80,256]{2,1,0:T(8,128)(2,1)S(1)} custom-call(bf16[512,2048]{1,0:T(8,128)(2,1)} %rows_ref.1, f32[1,2048]{1,0:T(1,128)} %bitcast.8, bf16[4,256,2048]{2,1,0:T(8,128)(2,1)} %bitcast.6), custom_call_target="tpu_custom_call" | custom-call | flops 335544320 | bytes 2359296 | tf_op jit(solution)/shard_map/pallas_call | solution.py:48
  2.7 3.0 %collective-permute-start = (bf16[4,80,256]{2,1,0:T(8,128)(2,1)S(1)}, bf16[4,80,256]{2,1,0:T(8,128)(2,1)S(1)}, u32[]{:S(2)}, u32[]{:S(2)}) collective-permute-start(bf16[4,80,256]{2,1,0:T(8,128)(2,1)S(1)} %shard_map.65._), channel_id=1, source_target_pairs={{0,16},{16,0},{1,17},{17,1},{2,18},{18,2},{3,19},{19,3},{4,20},{20... | collective-permute-start | bytes 491528 | tf_op jit(solution)/shard_map/ppermute | solution.py:223
  5.7 2.1 %shard_map.66 = (f32[4,80,256]{2,1,0:T(8,128)S(1)}, f32[4,112,256]{2,1,0:T(8,128)S(1)}, bf16[4,112,256]{2,1,0:T(8,128)(2,1)S(1)}, f32[4,64,256]{2,1,0:T(8,128)S(1)}, bf16[4,64,256]{2,1,0:T(8,128)(2,1)S(1)}) custom-call(bf16[512,2048]{1,0:T(8,128)(2,1)S(1)} %copy-done.1, f32[1,2048]{1,0:T(1,128)S(1)} %bitcast.9, bf16[4,256,2048]{2,1,0:T(8,128)(2,1)S(1)} %bitcast.7, ...), custom_call_target="tpu_custom_call" | custom-call | flops 2147483648 | bytes 6291456 | tf_op jit(solution)/shard_map/pallas_call | solution.py:93
  7.8 0.9 %collective-permute-start.3 = (bf16[4,112,256]{2,1,0:T(8,128)(2,1)S(1)}, bf16[4,112,256]{2,1,0:T(8,128)(2,1)S(1)}, u32[]{:S(2)}, u32[]{:S(2)}) collective-permute-start(bf16[4,112,256]{2,1,0:T(8,128)(2,1)S(1)} %get-tuple-element.26), channel_id=1, source_target_pairs={{0,16},{16,0},{1,17},{17,1},{2,18},{18,2},{3,19},{19,3},{4,20},{20... | collective-permute-start | bytes 688136 | tf_op jit(solution)/shard_map/ppermute | solution.py:223
  8.7 0.1 copy.7.picks_ref
  8.8 0.6 %shard_map.64.lists_ref = s32[8,8,256]{2,1,0:T(8,128)S(1)} custom-call(s32[4,2]{1,0:T(4,128)S(1)} %copy.7.picks_ref), custom_call_target="tpu_custom_call" | custom-call | tf_op jit(solution)/shard_map/pallas_call | solution.py:120
  9.4 0.6 %collective-permute-done.refs_0_ = bf16[4,80,256]{2,1,0:T(8,128)(2,1)S(1)} collective-permute-done((bf16[4,80,256]{2,1,0:T(8,128)(2,1)S(1)}, bf16[4,80,256]{2,1,0:T(8,128)(2,1)S(1)}, u32[]{:S(2)}, u32[]{:S(2)}) %collective-permute-start) | collective-permute-done | bytes 163872 | tf_op jit(solution)/shard_map/ppermute | solution.py:223
  9.9 0.1 shard_map.67
  10.0 1.9 %collective-permute-start.1 = (bf16[2,80,256]{2,1,0:T(8,128)(2,1)S(1)}, bf16[2,80,256]{2,1,0:T(8,128)(2,1)S(1)}, u32[]{:S(2)}, u32[]{:S(2)}) collective-permute-start(bf16[2,80,256]{2,1,0:T(8,128)(2,1)S(1)} %get-tuple-element.23), channel_id=1, source_target_pairs={{0,8},{4,12},{8,0},{12,4},{1,9},{5,13},{9,1},{13,5},{2,10},{6,14},... | collective-permute-start | bytes 245768 | tf_op jit(solution)/shard_map/ppermute | solution.py:223
  11.9 1.9 %collective-permute-start.6 = (bf16[4,64,256]{2,1,0:T(8,128)(2,1)S(1)}, bf16[4,64,256]{2,1,0:T(8,128)(2,1)S(1)}, u32[]{:S(2)}, u32[]{:S(2)}) collective-permute-start(bf16[4,64,256]{2,1,0:T(8,128)(2,1)S(1)} %get-tuple-element.33), channel_id=1, source_target_pairs={{0,16},{16,0},{1,17},{17,1},{2,18},{18,2},{3,19},{19,3},{4,20},{20... | collective-permute-start | bytes 393224 | tf_op jit(solution)/shard_map/ppermute | solution.py:223
  13.9 1.1 %collective-permute-done.3.refs_0_ = bf16[4,112,256]{2,1,0:T(8,128)(2,1)S(1)} collective-permute-done((bf16[4,112,256]{2,1,0:T(8,128)(2,1)S(1)}, bf16[4,112,256]{2,1,0:T(8,128)(2,1)S(1)}, u32[]{:S(2)}, u32[]{:S(2)}) %collective-permute-start.3) | collective-permute-done | bytes 229408 | tf_op jit(solution)/shard_map/ppermute | solution.py:223
  14.9 0.1 shard_map.68
  15.1 1.7 %collective-permute-start.4 = (bf16[2,112,256]{2,1,0:T(8,128)(2,1)S(1)}, bf16[2,112,256]{2,1,0:T(8,128)(2,1)S(1)}, u32[]{:S(2)}, u32[]{:S(2)}) collective-permute-start(bf16[2,112,256]{2,1,0:T(8,128)(2,1)S(1)} %get-tuple-element.29), channel_id=1, source_target_pairs={{0,8},{4,12},{8,0},{12,4},{1,9},{5,13},{9,1},{13,5},{2,10},{6,14},... | collective-permute-start | bytes 344072 | tf_op jit(solution)/shard_map/ppermute | solution.py:223
  16.9 0.2 shard_map.69.refs_1_.before_ref
  17.1 1.0 %collective-permute-done.6.refs_0_ = bf16[4,64,256]{2,1,0:T(8,128)(2,1)S(1)} collective-permute-done((bf16[4,64,256]{2,1,0:T(8,128)(2,1)S(1)}, bf16[4,64,256]{2,1,0:T(8,128)(2,1)S(1)}, u32[]{:S(2)}, u32[]{:S(2)}) %collective-permute-start.6) | collective-permute-done | bytes 131104 | tf_op jit(solution)/shard_map/ppermute | solution.py:223
  18.2 0.2 shard_map.71
  18.5 1.1 %collective-permute-start.8 = (bf16[2,64,256]{2,1,0:T(8,128)(2,1)S(1)}, bf16[2,64,256]{2,1,0:T(8,128)(2,1)S(1)}, u32[]{:S(2)}, u32[]{:S(2)}) collective-permute-start(bf16[2,64,256]{2,1,0:T(8,128)(2,1)S(1)} %get-tuple-element.37), channel_id=1, source_target_pairs={{0,8},{4,12},{8,0},{12,4},{1,9},{5,13},{9,1},{13,5},{2,10},{6,14},... | collective-permute-start | bytes 196616 | tf_op jit(solution)/shard_map/ppermute | solution.py:223
  19.6 0.7 %collective-permute-start.9 = (bf16[2,64,256]{2,1,0:T(8,128)(2,1)S(1)}, bf16[2,64,256]{2,1,0:T(8,128)(2,1)S(1)}, u32[]{:S(2)}, u32[]{:S(2)}) collective-permute-start(bf16[2,64,256]{2,1,0:T(8,128)(2,1)S(1)} %get-tuple-element.38), channel_id=1, source_target_pairs={{0,12},{4,8},{8,4},{12,0},{1,13},{5,9},{9,5},{13,1},{2,14},{6,10},... | collective-permute-start | bytes 196616 | tf_op jit(solution)/shard_map/ppermute | solution.py:223
  20.4 2.2 %collective-permute-done.5.refs_1_ = bf16[2,112,256]{2,1,0:T(8,128)(2,1)S(1)} collective-permute-done((bf16[2,112,256]{2,1,0:T(8,128)(2,1)S(1)}, bf16[2,112,256]{2,1,0:T(8,128)(2,1)S(1)}, u32[]{:S(2)}, u32[]{:S(2)}) %collective-permute-start.5) | collective-permute-done | bytes 114720 | tf_op jit(solution)/shard_map/ppermute | solution.py:223
  22.5 0.2 shard_map.72.before_ref
  22.8 0.3 %shard_map.73.before_ref = f32[1,256]{1,0:T(1,128)S(1)} custom-call(f32[1,256]{1,0:T(1,128)S(1)} %shard_map.72.before_ref, bf16[8,256,256]{2,1,0:T(8,128)(2,1)S(1)} %bitcast.12, bf16[8,256,256]{2,1,0:T(8,128)(2,1)S(1)} %bitcast.16, bf16[2,256,256]{2,1,0:T(8,128)(2,1)S(1)} %get-tuple-element.35.refs_2_.refs_0_, ...), custom_call_target="tpu_custom_call" | custom-call | flops 3000000000 | bytes 524288 | tf_op jit(solution)/shard_map/pallas_call | solution.py:208
  23.1 0.8 %collective-permute-done.8.refs_0_ = bf16[2,64,256]{2,1,0:T(8,128)(2,1)S(1)} collective-permute-done((bf16[2,64,256]{2,1,0:T(8,128)(2,1)S(1)}, bf16[2,64,256]{2,1,0:T(8,128)(2,1)S(1)}, u32[]{:S(2)}, u32[]{:S(2)}) %collective-permute-start.8) | collective-permute-done | bytes 65568 | tf_op jit(solution)/shard_map/ppermute | solution.py:223
  23.9 1.2 %collective-permute-done.9.refs_1_ = bf16[2,64,256]{2,1,0:T(8,128)(2,1)S(1)} collective-permute-done((bf16[2,64,256]{2,1,0:T(8,128)(2,1)S(1)}, bf16[2,64,256]{2,1,0:T(8,128)(2,1)S(1)}, u32[]{:S(2)}, u32[]{:S(2)}) %collective-permute-start.9) | collective-permute-done | bytes 65568 | tf_op jit(solution)/shard_map/ppermute | solution.py:223
  25.1 0.8 %shard_map.74 = f32[1,256]{1,0:T(1,128)} custom-call(f32[1,256]{1,0:T(1,128)S(1)} %shard_map.73.before_ref, bf16[8,256,256]{2,1,0:T(8,128)(2,1)S(1)} %bitcast.13, bf16[8,256,256]{2,1,0:T(8,128)(2,1)S(1)} %bitcast.17, bf16[2,64,256]{2,1,0:T(8,128)(2,1)S(1)} %collective-permute-done.8.refs_0_, bf16[2,64,256]{2,1,0:T(8,128)(2,1)S(1)} %collective-permute-done.9.refs_1_), custom_call_target="tpu_custom_call" | custom-call | flops 3000000000 | bytes 524288 | tf_op jit(solution)/shard_map/pallas_call | solution.py:208
  (21 shorter events, 0.2 us)
Async XLA Ops:
  0.0 5.7 %copy-start.2 = (f32[2048]{0:T(1024)S(1)}, f32[2048]{0:T(1024)}, u32[]{:S(2)}) copy-start(f32[2048]{0:T(1024)} %param.8) | copy-start | bytes 24580
  0.0 5.7 %copy-start = (bf16[1024,2048]{1,0:T(8,128)(2,1)S(1)}, bf16[1024,2048]{1,0:T(8,128)(2,1)}, u32[]{:S(2)}) copy-start(bf16[1024,2048]{1,0:T(8,128)(2,1)} %param.7) | copy-start | bytes 12582916
  0.0 5.7 %copy-start.1 = (bf16[512,2048]{1,0:T(8,128)(2,1)S(1)}, bf16[512,2048]{1,0:T(8,128)(2,1)}, u32[]{:S(2)}) copy-start(bf16[512,2048]{1,0:T(8,128)(2,1)} %rows_ref.1) | copy-start | bytes 6291460
  2.7 6.0 %copy-start.5 = (s32[1,1,1,4,2]{3,4,2,1,0:T(2,128)S(1)}, s32[1,1,1,4,2]{3,4,2,1,0:T(2,128)}, u32[]{:S(2)}) copy-start(s32[1,1,1,4,2]{3,4,2,1,0:T(2,128)} %param.9) | copy-start | bytes 100
  2.7 7.2 %collective-permute-start = (bf16[4,80,256]{2,1,0:T(8,128)(2,1)S(1)}, bf16[4,80,256]{2,1,0:T(8,128)(2,1)S(1)}, u32[]{:S(2)}, u32[]{:S(2)}) collective-permute-start(bf16[4,80,256]{2,1,0:T(8,128)(2,1)S(1)} %shard_map.65._), channel_id=1, source_target_pairs={{0,16},{16,0},{1,17},{17,1},{2,18},{18,2},{3,19},{19,3},{4,20},{20... | collective-permute-start | bytes 491528 | tf_op jit(solution)/shard_map/ppermute | solution.py:223
  7.8 7.1 %collective-permute-start.3 = (bf16[4,112,256]{2,1,0:T(8,128)(2,1)S(1)}, bf16[4,112,256]{2,1,0:T(8,128)(2,1)S(1)}, u32[]{:S(2)}, u32[]{:S(2)}) collective-permute-start(bf16[4,112,256]{2,1,0:T(8,128)(2,1)S(1)} %get-tuple-element.26), channel_id=1, source_target_pairs={{0,16},{16,0},{1,17},{17,1},{2,18},{18,2},{3,19},{19,3},{4,20},{20... | collective-permute-start | bytes 688136 | tf_op jit(solution)/shard_map/ppermute | solution.py:223
  10.0 6.8 %collective-permute-start.1 = (bf16[2,80,256]{2,1,0:T(8,128)(2,1)S(1)}, bf16[2,80,256]{2,1,0:T(8,128)(2,1)S(1)}, u32[]{:S(2)}, u32[]{:S(2)}) collective-permute-start(bf16[2,80,256]{2,1,0:T(8,128)(2,1)S(1)} %get-tuple-element.23), channel_id=1, source_target_pairs={{0,8},{4,12},{8,0},{12,4},{1,9},{5,13},{9,1},{13,5},{2,10},{6,14},... | collective-permute-start | bytes 245768 | tf_op jit(solution)/shard_map/ppermute | solution.py:223
  11.9 4.9 %collective-permute-start.2 = (bf16[2,80,256]{2,1,0:T(8,128)(2,1)S(1)}, bf16[2,80,256]{2,1,0:T(8,128)(2,1)S(1)}, u32[]{:S(2)}, u32[]{:S(2)}) collective-permute-start(bf16[2,80,256]{2,1,0:T(8,128)(2,1)S(1)} %get-tuple-element.24), channel_id=1, source_target_pairs={{0,12},{4,8},{8,4},{12,0},{1,13},{5,9},{9,5},{13,1},{2,14},{6,10},... | collective-permute-start | bytes 245768 | tf_op jit(solution)/shard_map/ppermute | solution.py:223
  11.9 6.2 %collective-permute-start.6 = (bf16[4,64,256]{2,1,0:T(8,128)(2,1)S(1)}, bf16[4,64,256]{2,1,0:T(8,128)(2,1)S(1)}, u32[]{:S(2)}, u32[]{:S(2)}) collective-permute-start(bf16[4,64,256]{2,1,0:T(8,128)(2,1)S(1)} %get-tuple-element.33), channel_id=1, source_target_pairs={{0,16},{16,0},{1,17},{17,1},{2,18},{18,2},{3,19},{19,3},{4,20},{20... | collective-permute-start | bytes 393224 | tf_op jit(solution)/shard_map/ppermute | solution.py:223
  14.9 1.9 %copy-start.3 = (bf16[1,1,1,8,256,256]{5,4,3,2,1,0:T(8,128)(2,1)S(1)}, bf16[1,1,1,8,256,256]{5,4,3,2,1,0:T(8,128)(2,1)}, u32[]{:S(2)}) copy-start(bf16[1,1,1,8,256,256]{5,4,3,2,1,0:T(8,128)(2,1)} %param.10) | copy-start | bytes 3145732
  14.9 1.9 %copy-start.4 = (bf16[1,1,1,8,256,256]{5,4,3,2,1,0:T(8,128)(2,1)S(1)}, bf16[1,1,1,8,256,256]{5,4,3,2,1,0:T(8,128)(2,1)}, u32[]{:S(2)}) copy-start(bf16[1,1,1,8,256,256]{5,4,3,2,1,0:T(8,128)(2,1)} %param.11) | copy-start | bytes 3145732
  15.1 5.3 %collective-permute-start.4 = (bf16[2,112,256]{2,1,0:T(8,128)(2,1)S(1)}, bf16[2,112,256]{2,1,0:T(8,128)(2,1)S(1)}, u32[]{:S(2)}, u32[]{:S(2)}) collective-permute-start(bf16[2,112,256]{2,1,0:T(8,128)(2,1)S(1)} %get-tuple-element.29), channel_id=1, source_target_pairs={{0,8},{4,12},{8,0},{12,4},{1,9},{5,13},{9,1},{13,5},{2,10},{6,14},... | collective-permute-start | bytes 344072 | tf_op jit(solution)/shard_map/ppermute | solution.py:223
  16.8 5.7 %collective-permute-start.5 = (bf16[2,112,256]{2,1,0:T(8,128)(2,1)S(1)}, bf16[2,112,256]{2,1,0:T(8,128)(2,1)S(1)}, u32[]{:S(2)}, u32[]{:S(2)}) collective-permute-start(bf16[2,112,256]{2,1,0:T(8,128)(2,1)S(1)} %get-tuple-element.30), channel_id=1, source_target_pairs={{0,12},{4,8},{8,4},{12,0},{1,13},{5,9},{9,5},{13,1},{2,14},{6,10},... | collective-permute-start | bytes 344072 | tf_op jit(solution)/shard_map/ppermute | solution.py:223
  18.4 4.4 %collective-permute-start.7 = (bf16[2,256,256]{2,1,0:T(8,128)(2,1)S(1)}, bf16[2,256,256]{2,1,0:T(8,128)(2,1)S(1)}, u32[]{:S(2)}, u32[]{:S(2)}) collective-permute-start(bf16[2,256,256]{2,1,0:T(8,128)(2,1)S(1)} %get-tuple-element.36), channel_id=1, source_target_pairs={{0,4},{4,0},{8,12},{12,8},{1,5},{5,1},{9,13},{13,9},{2,6},{6,2},{1... | collective-permute-start | bytes 786440 | tf_op jit(solution)/shard_map/ppermute | solution.py:223
  18.5 5.4 %collective-permute-start.8 = (bf16[2,64,256]{2,1,0:T(8,128)(2,1)S(1)}, bf16[2,64,256]{2,1,0:T(8,128)(2,1)S(1)}, u32[]{:S(2)}, u32[]{:S(2)}) collective-permute-start(bf16[2,64,256]{2,1,0:T(8,128)(2,1)S(1)} %get-tuple-element.37), channel_id=1, source_target_pairs={{0,8},{4,12},{8,0},{12,4},{1,9},{5,13},{9,1},{13,5},{2,10},{6,14},... | collective-permute-start | bytes 196616 | tf_op jit(solution)/shard_map/ppermute | solution.py:223
  19.6 5.4 %collective-permute-start.9 = (bf16[2,64,256]{2,1,0:T(8,128)(2,1)S(1)}, bf16[2,64,256]{2,1,0:T(8,128)(2,1)S(1)}, u32[]{:S(2)}, u32[]{:S(2)}) collective-permute-start(bf16[2,64,256]{2,1,0:T(8,128)(2,1)S(1)} %get-tuple-element.38), channel_id=1, source_target_pairs={{0,12},{4,8},{8,4},{12,0},{1,13},{5,9},{9,5},{13,1},{2,14},{6,10},... | collective-permute-start | bytes 196616 | tf_op jit(solution)/shard_map/ppermute | solution.py:223

commit v5 on v4

--- a/solution.py
+++ b/solution.py
@@ -11,7 +11,6 @@
 MIB = 1024 * 1024
 NT = (((1,), (1,)), ((), ()))
 VMEM = pl.BlockSpec(memory_space=pltpu.VMEM)
-SMEM = pl.BlockSpec(memory_space=pltpu.SMEM)
 HBM = pl.BlockSpec(memory_space=pltpu.HBM)
 ANY = pl.BlockSpec(memory_space=pl.ANY)
 NEAR = 2
@@ -108,24 +107,6 @@
     return dict(zip(keys, outs))
 
 
-def spread_kernel(picks_ref, out):
-    owners, slots = picks_ref.shape
-    row = lax.axis_index("row")
-    for d in range(owners):
-        for k in range(slots):
-            out[d * slots + k] = jnp.full(out.shape[1:], picks_ref[row ^ d, k], jnp.int32)
-
-
-def spread(picks, side):
-    return pl.pallas_call(
-        spread_kernel,
-        in_specs=[SMEM],
-        out_specs=VMEM,
-        out_shape=jax.ShapeDtypeStruct((picks.size, 8, side), jnp.int32),
-        compiler_params=params(8),
-    )(picks)
-
-
 def listed_tile(listed, tiles):
     chosen = jnp.zeros_like(tiles[0])
     for t, tile in enumerate(tiles):
@@ -135,6 +116,7 @@
 
 def pick_kernel(groups, far, slots, lists_ref, own_ref, *refs):
     parts, tiles_ref, outs = refs[: groups - 1], refs[-1 - far], refs[-far:]
+    row = lax.axis_index("row")
     tiles = []
     for t in range(own_ref.shape[0]):
         total = own_ref[t]
@@ -144,7 +126,7 @@
         tiles_ref[t] = total.astype(jnp.bfloat16)
     for d, out in enumerate(outs, NEAR):
         for k in range(slots):
-            out[k] = listed_tile(lists_ref[d * slots + k, :1], tiles)
+            out[k] = listed_tile(lists_ref[(row ^ d) * slots + k, :1], tiles)
 
 
 def pick(lists, slots, own, parts, after):
@@ -165,13 +147,14 @@
 
 def near_kernel(slots, lists_ref, *refs):
     chunks, outs = refs[:-NEAR], refs[-NEAR:]
+    row = lax.axis_index("row")
     start = 0
     for chunk in chunks:
         count, height, side = chunk.shape
         tiles = [chunk[t].astype(jnp.float32) for t in range(count)]
         for d, out in enumerate(outs):
             for k in range(slots):
-                out[k, start : start + height] = listed_tile(lists_ref[d * slots + k, :1], tiles)
+                out[k, start : start + height] = listed_tile(lists_ref[(row ^ d) * slots + k, :1], tiles)
         start += height
 
 
@@ -231,7 +214,7 @@
     row_phi, col_phi, picks = row_phi[0, 0, 0], col_phi[0, 0, 0], send_list[0, 0, 0]
     factors = coeff_rows, occupation[None, :], coeff_cols.reshape(-1, side, coeff_cols.shape[1]), side
 
-    lists = spread(picks, side)
+    lists = jnp.broadcast_to(picks.reshape(-1, 1, 1), (picks.size, 8, side))
     early = first(heights[0], *factors)
     parts = rest(heights, *factors, early)
     parts[0, 1] = early

time: 26 us -> 26 us (level)
  Pallas kernels: 7.48 us -> 6.89 us
  waiting for transfers between devices: 6.75 us -> 7.19 us
    pallas_call x1 -> x0, Pallas kernels: 0.58 us -> none  [spread(): pl.pallas_call(spread_kernel, in_specs=[SMEM], out_specs=VMEM, out_shape=...]
    ppermute x10, waiting for transfers between devices: 6.75 us -> 7.19 us  [swap(): lax.ppermute(value, axis, [(i, i ^ d) for i in range(lax.axis_size(axis))])]
  transfers between devices with their start and end apart: 10 -> 10, of which waited for: 6 -> 6; matrix products, arithmetic and copies ran while one was open for 0% -> 1% of each run, Pallas kernels for 15% -> 13%
where the time goes in v5:
time: 26 us; the launch traced here: 25.9 us
  starting transfers between devices  11.4 us (44%)
  waiting for transfers between devices  7.19 us (28%)
  Pallas kernels  6.89 us (26%)
  local copies, waits for them, and re-layouts  0.28 us (1%)
    ppermute x10, starting transfers between devices, swap(): lax.ppermute(value, axis, [(i, i ^ d) for i in range(lax.axis_size(axis))])  11.4 us
    ppermute x10, waiting for transfers between devices, swap(): lax.ppermute(value, axis, [(i, i ^ d) for i in range(lax.axis_size(axis))])  7.19 us
    pallas_call x1, Pallas kernels, first(): pl.pallas_call(first_kernel, in_specs=[HBM] * 3, out_specs=VMEM, out_shap...  2.69 us
    pallas_call x1, Pallas kernels, rest(): pl.pallas_call(functools.partial(rest_kernel, heights), in_specs=[VMEM] *...  2.07 us
    pallas_call x4, Pallas kernels, contract(): pl.pallas_call(functools.partial(contract_kernel, base, len(gots), start)...  1.59 us
  transfers between devices with their start and end apart: 10, of which 6 were waited for; matrix products, arithmetic and copies ran while one was open for 1% of the time, Pallas kernels for 13%

profile of v5, /device:TPU:0, one launch (start us, length us, event | category | flops | bytes accessed | tf_op | source)
XLA Modules:
  0.0 25.9 jit_solution(14877665771679451799)
XLA Ops:
  0.0 2.7 %shard_map.64._ = bf16[4,80,256]{2,1,0:T(8,128)(2,1)S(1)} custom-call(bf16[512,2048]{1,0:T(8,128)(2,1)} %rows_ref.1, f32[1,2048]{1,0:T(1,128)} %bitcast.7, bf16[4,256,2048]{2,1,0:T(8,128)(2,1)} %bitcast.5), custom_call_target="tpu_custom_call" | custom-call | flops 335544320 | bytes 2359296 | tf_op jit(solution)/shard_map/pallas_call | solution.py:47
  2.7 3.0 %collective-permute-start = (bf16[4,80,256]{2,1,0:T(8,128)(2,1)S(1)}, bf16[4,80,256]{2,1,0:T(8,128)(2,1)S(1)}, u32[]{:S(2)}, u32[]{:S(2)}) collective-permute-start(bf16[4,80,256]{2,1,0:T(8,128)(2,1)S(1)} %shard_map.64._), channel_id=1, source_target_pairs={{0,16},{16,0},{1,17},{17,1},{2,18},{18,2},{3,19},{19,3},{4,20},{20... | collective-permute-start | bytes 491528 | tf_op jit(solution)/shard_map/ppermute | solution.py:206
  5.7 2.1 %shard_map.65 = (f32[4,80,256]{2,1,0:T(8,128)S(1)}, f32[4,112,256]{2,1,0:T(8,128)S(1)}, bf16[4,112,256]{2,1,0:T(8,128)(2,1)S(1)}, f32[4,64,256]{2,1,0:T(8,128)S(1)}, bf16[4,64,256]{2,1,0:T(8,128)(2,1)S(1)}) custom-call(bf16[512,2048]{1,0:T(8,128)(2,1)S(1)} %copy-done.1, f32[1,2048]{1,0:T(1,128)S(1)} %bitcast.8, bf16[4,256,2048]{2,1,0:T(8,128)(2,1)S(1)} %bitcast.6, ...), custom_call_target="tpu_custom_call" | custom-call | flops 2147483648 | bytes 6291456 | tf_op jit(solution)/shard_map/pallas_call | solution.py:92
  7.8 0.9 %collective-permute-start.3 = (bf16[4,112,256]{2,1,0:T(8,128)(2,1)S(1)}, bf16[4,112,256]{2,1,0:T(8,128)(2,1)S(1)}, u32[]{:S(2)}, u32[]{:S(2)}) collective-permute-start(bf16[4,112,256]{2,1,0:T(8,128)(2,1)S(1)} %get-tuple-element.26), channel_id=1, source_target_pairs={{0,16},{16,0},{1,17},{17,1},{2,18},{18,2},{3,19},{19,3},{4,20},{20... | collective-permute-start | bytes 688136 | tf_op jit(solution)/shard_map/ppermute | solution.py:206
  8.7 0.1 copy.8
  8.8 0.1 broadcast_in_dim.14
  8.9 1.1 %collective-permute-done.refs_0_ = bf16[4,80,256]{2,1,0:T(8,128)(2,1)S(1)} collective-permute-done((bf16[4,80,256]{2,1,0:T(8,128)(2,1)S(1)}, bf16[4,80,256]{2,1,0:T(8,128)(2,1)S(1)}, u32[]{:S(2)}, u32[]{:S(2)}) %collective-permute-start) | collective-permute-done | bytes 163872 | tf_op jit(solution)/shard_map/ppermute | solution.py:206
  10.0 0.1 shard_map.66
  10.1 1.9 %collective-permute-start.1 = (bf16[2,80,256]{2,1,0:T(8,128)(2,1)S(1)}, bf16[2,80,256]{2,1,0:T(8,128)(2,1)S(1)}, u32[]{:S(2)}, u32[]{:S(2)}) collective-permute-start(bf16[2,80,256]{2,1,0:T(8,128)(2,1)S(1)} %get-tuple-element.23), channel_id=1, source_target_pairs={{0,8},{4,12},{8,0},{12,4},{1,9},{5,13},{9,1},{13,5},{2,10},{6,14},... | collective-permute-start | bytes 245768 | tf_op jit(solution)/shard_map/ppermute | solution.py:206
  12.0 1.9 %collective-permute-start.6 = (bf16[4,64,256]{2,1,0:T(8,128)(2,1)S(1)}, bf16[4,64,256]{2,1,0:T(8,128)(2,1)S(1)}, u32[]{:S(2)}, u32[]{:S(2)}) collective-permute-start(bf16[4,64,256]{2,1,0:T(8,128)(2,1)S(1)} %get-tuple-element.33), channel_id=1, source_target_pairs={{0,16},{16,0},{1,17},{17,1},{2,18},{18,2},{3,19},{19,3},{4,20},{20... | collective-permute-start | bytes 393224 | tf_op jit(solution)/shard_map/ppermute | solution.py:206
  13.9 1.0 %collective-permute-done.3.refs_0_ = bf16[4,112,256]{2,1,0:T(8,128)(2,1)S(1)} collective-permute-done((bf16[4,112,256]{2,1,0:T(8,128)(2,1)S(1)}, bf16[4,112,256]{2,1,0:T(8,128)(2,1)S(1)}, u32[]{:S(2)}, u32[]{:S(2)}) %collective-permute-start.3) | collective-permute-done | bytes 229408 | tf_op jit(solution)/shard_map/ppermute | solution.py:206
  14.9 0.1 shard_map.67
  15.1 1.7 %collective-permute-start.4 = (bf16[2,112,256]{2,1,0:T(8,128)(2,1)S(1)}, bf16[2,112,256]{2,1,0:T(8,128)(2,1)S(1)}, u32[]{:S(2)}, u32[]{:S(2)}) collective-permute-start(bf16[2,112,256]{2,1,0:T(8,128)(2,1)S(1)} %get-tuple-element.29), channel_id=1, source_target_pairs={{0,8},{4,12},{8,0},{12,4},{1,9},{5,13},{9,1},{13,5},{2,10},{6,14},... | collective-permute-start | bytes 344072 | tf_op jit(solution)/shard_map/ppermute | solution.py:206
  16.9 0.2 shard_map.68.refs_1_.before_ref
  17.1 1.1 %collective-permute-done.6.refs_0_ = bf16[4,64,256]{2,1,0:T(8,128)(2,1)S(1)} collective-permute-done((bf16[4,64,256]{2,1,0:T(8,128)(2,1)S(1)}, bf16[4,64,256]{2,1,0:T(8,128)(2,1)S(1)}, u32[]{:S(2)}, u32[]{:S(2)}) %collective-permute-start.6) | collective-permute-done | bytes 131104 | tf_op jit(solution)/shard_map/ppermute | solution.py:206
  18.3 0.2 shard_map.70
  18.6 1.0 %collective-permute-start.8 = (bf16[2,64,256]{2,1,0:T(8,128)(2,1)S(1)}, bf16[2,64,256]{2,1,0:T(8,128)(2,1)S(1)}, u32[]{:S(2)}, u32[]{:S(2)}) collective-permute-start(bf16[2,64,256]{2,1,0:T(8,128)(2,1)S(1)} %get-tuple-element.37), channel_id=1, source_target_pairs={{0,8},{4,12},{8,0},{12,4},{1,9},{5,13},{9,1},{13,5},{2,10},{6,14},... | collective-permute-start | bytes 196616 | tf_op jit(solution)/shard_map/ppermute | solution.py:206
  19.6 0.8 %collective-permute-start.9 = (bf16[2,64,256]{2,1,0:T(8,128)(2,1)S(1)}, bf16[2,64,256]{2,1,0:T(8,128)(2,1)S(1)}, u32[]{:S(2)}, u32[]{:S(2)}) collective-permute-start(bf16[2,64,256]{2,1,0:T(8,128)(2,1)S(1)} %get-tuple-element.38), channel_id=1, source_target_pairs={{0,12},{4,8},{8,4},{12,0},{1,13},{5,9},{9,5},{13,1},{2,14},{6,10},... | collective-permute-start | bytes 196616 | tf_op jit(solution)/shard_map/ppermute | solution.py:206
  20.5 2.2 %collective-permute-done.5.refs_1_ = bf16[2,112,256]{2,1,0:T(8,128)(2,1)S(1)} collective-permute-done((bf16[2,112,256]{2,1,0:T(8,128)(2,1)S(1)}, bf16[2,112,256]{2,1,0:T(8,128)(2,1)S(1)}, u32[]{:S(2)}, u32[]{:S(2)}) %collective-permute-start.5) | collective-permute-done | bytes 114720 | tf_op jit(solution)/shard_map/ppermute | solution.py:206
  22.6 0.2 shard_map.71.before_ref
  22.9 0.3 %shard_map.72.before_ref = f32[1,256]{1,0:T(1,128)S(1)} custom-call(f32[1,256]{1,0:T(1,128)S(1)} %shard_map.71.before_ref, bf16[8,256,256]{2,1,0:T(8,128)(2,1)S(1)} %bitcast.11, bf16[8,256,256]{2,1,0:T(8,128)(2,1)S(1)} %bitcast.15, bf16[2,256,256]{2,1,0:T(8,128)(2,1)S(1)} %get-tuple-element.35.refs_2_.refs_0_, ...), custom_call_target="tpu_custom_call" | custom-call | flops 3000000000 | bytes 524288 | tf_op jit(solution)/shard_map/pallas_call | solution.py:191
  23.2 0.7 %collective-permute-done.8.refs_0_ = bf16[2,64,256]{2,1,0:T(8,128)(2,1)S(1)} collective-permute-done((bf16[2,64,256]{2,1,0:T(8,128)(2,1)S(1)}, bf16[2,64,256]{2,1,0:T(8,128)(2,1)S(1)}, u32[]{:S(2)}, u32[]{:S(2)}) %collective-permute-start.8) | collective-permute-done | bytes 65568 | tf_op jit(solution)/shard_map/ppermute | solution.py:206
  23.9 1.2 %collective-permute-done.9.refs_1_ = bf16[2,64,256]{2,1,0:T(8,128)(2,1)S(1)} collective-permute-done((bf16[2,64,256]{2,1,0:T(8,128)(2,1)S(1)}, bf16[2,64,256]{2,1,0:T(8,128)(2,1)S(1)}, u32[]{:S(2)}, u32[]{:S(2)}) %collective-permute-start.9) | collective-permute-done | bytes 65568 | tf_op jit(solution)/shard_map/ppermute | solution.py:206
  25.1 0.8 %shard_map.73 = f32[1,256]{1,0:T(1,128)} custom-call(f32[1,256]{1,0:T(1,128)S(1)} %shard_map.72.before_ref, bf16[8,256,256]{2,1,0:T(8,128)(2,1)S(1)} %bitcast.12, bf16[8,256,256]{2,1,0:T(8,128)(2,1)S(1)} %bitcast.16, bf16[2,64,256]{2,1,0:T(8,128)(2,1)S(1)} %collective-permute-done.8.refs_0_, bf16[2,64,256]{2,1,0:T(8,128)(2,1)S(1)} %collective-permute-done.9.refs_1_), custom_call_target="tpu_custom_call" | custom-call | flops 3000000000 | bytes 524288 | tf_op jit(solution)/shard_map/pallas_call | solution.py:191
  (22 shorter events, 0.3 us)
Async XLA Ops:
  0.0 5.7 %copy-start.2 = (f32[2048]{0:T(1024)S(1)}, f32[2048]{0:T(1024)}, u32[]{:S(2)}) copy-start(f32[2048]{0:T(1024)} %param.8) | copy-start | bytes 24580
  0.0 5.7 %copy-start = (bf16[1024,2048]{1,0:T(8,128)(2,1)S(1)}, bf16[1024,2048]{1,0:T(8,128)(2,1)}, u32[]{:S(2)}) copy-start(bf16[1024,2048]{1,0:T(8,128)(2,1)} %param.7) | copy-start | bytes 12582916
  0.0 5.7 %copy-start.1 = (bf16[512,2048]{1,0:T(8,128)(2,1)S(1)}, bf16[512,2048]{1,0:T(8,128)(2,1)}, u32[]{:S(2)}) copy-start(bf16[512,2048]{1,0:T(8,128)(2,1)} %rows_ref.1) | copy-start | bytes 6291460
  2.7 6.0 %copy-start.5 = (s32[1,1,1,4,2]{3,4,2,1,0:T(2,128)S(1)}, s32[1,1,1,4,2]{3,4,2,1,0:T(2,128)}, u32[]{:S(2)}) copy-start(s32[1,1,1,4,2]{3,4,2,1,0:T(2,128)} %param.9) | copy-start | bytes 100
  2.7 7.2 %collective-permute-start = (bf16[4,80,256]{2,1,0:T(8,128)(2,1)S(1)}, bf16[4,80,256]{2,1,0:T(8,128)(2,1)S(1)}, u32[]{:S(2)}, u32[]{:S(2)}) collective-permute-start(bf16[4,80,256]{2,1,0:T(8,128)(2,1)S(1)} %shard_map.64._), channel_id=1, source_target_pairs={{0,16},{16,0},{1,17},{17,1},{2,18},{18,2},{3,19},{19,3},{4,20},{20... | collective-permute-start | bytes 491528 | tf_op jit(solution)/shard_map/ppermute | solution.py:206
  7.8 7.1 %collective-permute-start.3 = (bf16[4,112,256]{2,1,0:T(8,128)(2,1)S(1)}, bf16[4,112,256]{2,1,0:T(8,128)(2,1)S(1)}, u32[]{:S(2)}, u32[]{:S(2)}) collective-permute-start(bf16[4,112,256]{2,1,0:T(8,128)(2,1)S(1)} %get-tuple-element.26), channel_id=1, source_target_pairs={{0,16},{16,0},{1,17},{17,1},{2,18},{18,2},{3,19},{19,3},{4,20},{20... | collective-permute-start | bytes 688136 | tf_op jit(solution)/shard_map/ppermute | solution.py:206
  10.1 6.7 %collective-permute-start.1 = (bf16[2,80,256]{2,1,0:T(8,128)(2,1)S(1)}, bf16[2,80,256]{2,1,0:T(8,128)(2,1)S(1)}, u32[]{:S(2)}, u32[]{:S(2)}) collective-permute-start(bf16[2,80,256]{2,1,0:T(8,128)(2,1)S(1)} %get-tuple-element.23), channel_id=1, source_target_pairs={{0,8},{4,12},{8,0},{12,4},{1,9},{5,13},{9,1},{13,5},{2,10},{6,14},... | collective-permute-start | bytes 245768 | tf_op jit(solution)/shard_map/ppermute | solution.py:206
  12.0 4.8 %collective-permute-start.2 = (bf16[2,80,256]{2,1,0:T(8,128)(2,1)S(1)}, bf16[2,80,256]{2,1,0:T(8,128)(2,1)S(1)}, u32[]{:S(2)}, u32[]{:S(2)}) collective-permute-start(bf16[2,80,256]{2,1,0:T(8,128)(2,1)S(1)} %get-tuple-element.24), channel_id=1, source_target_pairs={{0,12},{4,8},{8,4},{12,0},{1,13},{5,9},{9,5},{13,1},{2,14},{6,10},... | collective-permute-start | bytes 245768 | tf_op jit(solution)/shard_map/ppermute | solution.py:206
  12.0 6.2 %collective-permute-start.6 = (bf16[4,64,256]{2,1,0:T(8,128)(2,1)S(1)}, bf16[4,64,256]{2,1,0:T(8,128)(2,1)S(1)}, u32[]{:S(2)}, u32[]{:S(2)}) collective-permute-start(bf16[4,64,256]{2,1,0:T(8,128)(2,1)S(1)} %get-tuple-element.33), channel_id=1, source_target_pairs={{0,16},{16,0},{1,17},{17,1},{2,18},{18,2},{3,19},{19,3},{4,20},{20... | collective-permute-start | bytes 393224 | tf_op jit(solution)/shard_map/ppermute | solution.py:206
  14.9 1.9 %copy-start.3 = (bf16[1,1,1,8,256,256]{5,4,3,2,1,0:T(8,128)(2,1)S(1)}, bf16[1,1,1,8,256,256]{5,4,3,2,1,0:T(8,128)(2,1)}, u32[]{:S(2)}) copy-start(bf16[1,1,1,8,256,256]{5,4,3,2,1,0:T(8,128)(2,1)} %param.10) | copy-start | bytes 3145732
  14.9 1.9 %copy-start.4 = (bf16[1,1,1,8,256,256]{5,4,3,2,1,0:T(8,128)(2,1)S(1)}, bf16[1,1,1,8,256,256]{5,4,3,2,1,0:T(8,128)(2,1)}, u32[]{:S(2)}) copy-start(bf16[1,1,1,8,256,256]{5,4,3,2,1,0:T(8,128)(2,1)} %param.11) | copy-start | bytes 3145732
  15.1 5.4 %collective-permute-start.4 = (bf16[2,112,256]{2,1,0:T(8,128)(2,1)S(1)}, bf16[2,112,256]{2,1,0:T(8,128)(2,1)S(1)}, u32[]{:S(2)}, u32[]{:S(2)}) collective-permute-start(bf16[2,112,256]{2,1,0:T(8,128)(2,1)S(1)} %get-tuple-element.29), channel_id=1, source_target_pairs={{0,8},{4,12},{8,0},{12,4},{1,9},{5,13},{9,1},{13,5},{2,10},{6,14},... | collective-permute-start | bytes 344072 | tf_op jit(solution)/shard_map/ppermute | solution.py:206
  16.8 5.8 %collective-permute-start.5 = (bf16[2,112,256]{2,1,0:T(8,128)(2,1)S(1)}, bf16[2,112,256]{2,1,0:T(8,128)(2,1)S(1)}, u32[]{:S(2)}, u32[]{:S(2)}) collective-permute-start(bf16[2,112,256]{2,1,0:T(8,128)(2,1)S(1)} %get-tuple-element.30), channel_id=1, source_target_pairs={{0,12},{4,8},{8,4},{12,0},{1,13},{5,9},{9,5},{13,1},{2,14},{6,10},... | collective-permute-start | bytes 344072 | tf_op jit(solution)/shard_map/ppermute | solution.py:206
  18.5 4.4 %collective-permute-start.7 = (bf16[2,256,256]{2,1,0:T(8,128)(2,1)S(1)}, bf16[2,256,256]{2,1,0:T(8,128)(2,1)S(1)}, u32[]{:S(2)}, u32[]{:S(2)}) collective-permute-start(bf16[2,256,256]{2,1,0:T(8,128)(2,1)S(1)} %get-tuple-element.36), channel_id=1, source_target_pairs={{0,4},{4,0},{8,12},{12,8},{1,5},{5,1},{9,13},{13,9},{2,6},{6,2},{1... | collective-permute-start | bytes 786440 | tf_op jit(solution)/shard_map/ppermute | solution.py:206
  18.6 5.3 %collective-permute-start.8 = (bf16[2,64,256]{2,1,0:T(8,128)(2,1)S(1)}, bf16[2,64,256]{2,1,0:T(8,128)(2,1)S(1)}, u32[]{:S(2)}, u32[]{:S(2)}) collective-permute-start(bf16[2,64,256]{2,1,0:T(8,128)(2,1)S(1)} %get-tuple-element.37), channel_id=1, source_target_pairs={{0,8},{4,12},{8,0},{12,4},{1,9},{5,13},{9,1},{13,5},{2,10},{6,14},... | collective-permute-start | bytes 196616 | tf_op jit(solution)/shard_map/ppermute | solution.py:206
  19.6 5.4 %collective-permute-start.9 = (bf16[2,64,256]{2,1,0:T(8,128)(2,1)S(1)}, bf16[2,64,256]{2,1,0:T(8,128)(2,1)S(1)}, u32[]{:S(2)}, u32[]{:S(2)}) collective-permute-start(bf16[2,64,256]{2,1,0:T(8,128)(2,1)S(1)} %get-tuple-element.38), channel_id=1, source_target_pairs={{0,12},{4,8},{8,4},{12,0},{1,13},{5,9},{9,5},{13,1},{2,14},{6,10},... | collective-permute-start | bytes 196616 | tf_op jit(solution)/shard_map/ppermute | solution.py:206
